TPU v7x, 32 devices: a whole 2x2x4 slice. The times are simulated.
32 devices in a mesh: tm: 4 (over y, x), stat: 8 (over z, core).
Axes of the slice: x: 2, y: 2, z: 4, core: 2. Of those that a mesh axis runs over, the one named last changes fastest.
Arguments:
- voltages: bfloat16 [512, 163840], P('stat', 'tm'), may hold values from -6 to 6
- taper: float32 [16, 4096], replicated, may hold values from -1.5 to 1.5
Outputs:
- visibility: float32 [4, 2, 512, 5, 64, 512], P('tm', None, 'stat')
All inputs are finite; a program needn't handle non-finite values.
Results may differ from a plain program's by a relative error of at most 0.0039.
Values may be sent and summed in bfloat16 or wider, within the bound.
A program may use at most 512 MiB of HBM per device.

v0:
```python
import math

import jax
import jax.numpy as jnp
from jax import lax
from jax.sharding import PartitionSpec as P

NSPEC = 25


def from_behind(value, axis, steps):
    count = lax.axis_size(axis)
    pairs = [(source, (source + steps) % count) for source in range(count)]
    return lax.ppermute(value, axis, pairs)


def dft_table(segment, channel_count, frame_len):
    sample_idx = jnp.arange(segment, dtype=jnp.int32)[:, None]
    channel_idx = jnp.arange(channel_count, dtype=jnp.int32)[None, :]
    angles = 2.0 * math.pi / segment * (sample_idx * channel_idx % segment).astype(jnp.float32)
    cosine = jnp.cos(angles)
    sine_part = jnp.sin(angles)
    upper = jnp.concatenate([cosine, -sine_part], axis=1)
    lower = jnp.concatenate([sine_part, cosine], axis=1)
    return jnp.concatenate([upper, lower], axis=0) / math.sqrt(frame_len)


def fold_twiddle(filtered, residue, tm_count, frame_len):
    row_count = filtered.shape[0]
    segment = frame_len // tm_count
    pieces = filtered.reshape(row_count, tm_count, segment)
    outer_idx = jnp.arange(tm_count, dtype=jnp.int32)
    outer_angles = 2.0 * math.pi / tm_count * (residue * outer_idx % tm_count).astype(jnp.float32)
    sum_real = jnp.sum(pieces * jnp.cos(outer_angles)[None, :, None], axis=1)
    sum_imag = -jnp.sum(pieces * jnp.sin(outer_angles)[None, :, None], axis=1)
    inner_idx = jnp.arange(segment, dtype=jnp.int32)
    inner_angles = 2.0 * math.pi / frame_len * (residue * inner_idx % frame_len).astype(jnp.float32)
    inner_cos = jnp.cos(inner_angles)[None, :]
    inner_sin = jnp.sin(inner_angles)[None, :]
    twisted_real = sum_real * inner_cos + sum_imag * inner_sin
    twisted_imag = sum_imag * inner_cos - sum_real * inner_sin
    return jnp.concatenate([twisted_real, twisted_imag], axis=1)


def polyphase(series, taper, spectra_count):
    row_count = series.shape[0]
    tap_count = taper.shape[0]
    frame_len = taper.shape[1]
    frames = series.reshape(row_count, spectra_count + tap_count - 1, frame_len)
    filtered = jnp.zeros((row_count, spectra_count, frame_len), jnp.float32)
    for tap_index in range(tap_count):
        filtered = filtered + taper[tap_index][None, None, :] * frames[
            :, tap_index : tap_index + spectra_count, :
        ].astype(jnp.float32)
    return filtered.reshape(row_count * spectra_count, frame_len)


def correlate(conjugated, partner_block, spectra_count):
    cross = jnp.einsum(
        "opisc,pmsc->oimc", conjugated, partner_block, preferred_element_type=jnp.float32
    )
    return cross / spectra_count


def shards(voltages, taper):
    tm_count = lax.axis_size("tm")
    stat_count = lax.axis_size("stat")
    tm_index = lax.axis_index("tm")
    local_inputs = voltages.shape[0]
    frame_len = taper.shape[1]
    segment = frame_len // tm_count
    channel_count = frame_len // 2 // tm_count
    spectra_count = NSPEC
    lag_count = stat_count // 2 + 1
    table = dft_table(segment, channel_count, frame_len)
    whole_series = lax.all_gather(voltages, "tm", axis=1, tiled=True)
    filtered = polyphase(whole_series, taper, spectra_count)
    twisted = fold_twiddle(filtered, tm_index, tm_count, frame_len)
    spectra = jnp.dot(
        twisted, table, precision=lax.Precision.HIGHEST, preferred_element_type=jnp.float32
    )
    spectra = spectra.reshape(local_inputs, spectra_count, 2, channel_count)
    own_block = jnp.transpose(spectra, (2, 0, 1, 3)).astype(jnp.bfloat16)
    conjugated = jnp.stack([own_block, jnp.stack([own_block[1], -own_block[0]])])
    visibility = jnp.zeros((2, local_inputs, lag_count, local_inputs, channel_count), jnp.float32)
    visibility = visibility.at[:, :, 0].set(correlate(conjugated, own_block, spectra_count))

    def lag_step(lag_index, carried):
        partner_block, accumulated = carried
        partner_block = from_behind(partner_block, "stat", -1)
        cross = correlate(conjugated, partner_block, spectra_count)
        accumulated = lax.dynamic_update_slice_in_dim(accumulated, cross[:, :, None], lag_index, 2)
        return (partner_block, accumulated)

    carried_out = lax.fori_loop(1, lag_count, lag_step, (own_block, visibility))
    visibility = carried_out[1]
    return visibility[None]


def solution(mesh):
    return jax.shard_map(
        shards,
        mesh=mesh,
        in_specs=(P("stat", "tm"), P()),
        out_specs=P("tm", None, "stat", None, None, None),
        check_vma=False,
    )
```

profile of v0, /device:TPU:0, one launch (start us, length us, event | category | flops | bytes accessed | tf_op | source)
XLA Modules:
  0.0 1070.3 jit_solution(5715505198837523400)
XLA Ops:
  26.7 178.3 %all-gather.2.cloned.1.call-done = bf16[64,163840]{1,0:T(8,128)(2,1)} async-done(((bf16[64,40960]{1,0:T(8,128)(2,1)}), bf16[64,163840]{1,0:T(8,128)(2,1)}) %all-gather.2.cloned.1.call-update) | async-done | bytes 20971536 | tf_op jit(solution)/shard_map/all_gather | solution.py:76
  205.0 22.7 %copy.22 = bf16[8,8,40,4096]{3,2,1,0:T(8,128)(2,1)} copy(bf16[8,8,40,4096]{3,1,2,0:T(8,128)(2,1)} %bitcast.68) | data formatting | bytes 41943040
  227.7 134.3 %multiply_add_fusion = f32[64,25,4096]{2,1,0:T(8,128)} fusion(bf16[64,40,4096]{2,1,0:T(8,128)(2,1)} %bitcast.66, f32[4096]{0:T(1024)S(1)} %bitcast.83, f32[4096]{0:T(1024)S(1)} %bitcast.84, f32[4096]{0:T(1024)S(1)} %bitcast.70, f32[4096]{0:T(1024)S(1)} %bitcast.71, f32[4096]{0:T(1024)S(1)} %bitcast.72, f32[4096]{0:T(1024)S(1)} %bitcast.73, ...), kind=kLoop, calls=%fused_computation.4 | loop fusion | flops 308019200 | bytes 236191744 | tf_op jit(solution)/shard_map/add | solution.py:52
  362.0 31.9 %reshape_reshape.3 = f32[1600,4,1024]{2,1,0:T(4,128)} reshape(f32[64,25,4096]{2,1,0:T(8,128)} %multiply_add_fusion) | data formatting | bytes 52428800 | tf_op jit(solution)/shard_map/reshape;reshape | solution.py:31
  393.9 45.7 %multiply_reduce_fusion = (f32[1600,1024]{1,0:T(8,128)}, f32[1600,1024]{1,0:T(8,128)}) fusion(f32[1600,4,1024]{2,1,0:T(4,128)} %reshape_reshape.3, f32[4]{0:T(128)S(1)} %get-tuple-element.166, f32[4]{0:T(128)S(1)} %get-tuple-element.167), kind=kLoop, calls=%fused_computation.5 | loop fusion | flops 22937600 | bytes 39321632 | tf_op jit(solution)/shard_map/reduce_sum | solution.py:35
  439.5 12.9 %multiply_add_fusion.1 = (f32[1600,1024]{1,0:T(8,128)}, f32[1600,1024]{1,0:T(8,128)}) fusion(f32[1600,1024]{1,0:T(8,128)} %get-tuple-element.133, f32[1600,1024]{1,0:T(8,128)} %get-tuple-element.132, f32[1024]{0:T(1024)S(1)} %get-tuple-element.164, f32[1024]{0:T(1024)S(1)} %get-tuple-element.165), kind=kLoop, calls=%fused_computation.21 | loop fusion | flops 11468800 | bytes 26222592 | tf_op jit(solution)/shard_map/add | solution.py:40
  452.4 48.6 %fusion.13 = bf16[1600,1024]{1,0:T(8,128)(2,1)} fusion(f32[1024,512]{1,0:T(8,128)} %get-tuple-element.169, f32[1024,512]{1,0:T(8,128)} %get-tuple-element.168, f32[1024,512]{1,0:T(8,128)S(1)} %fusion.24, f32[1600,1024]{1,0:T(8,128)} %get-tuple-element.143, f32[1600,1024]{1,0:T(8,128)} %get-tuple-element.142), kind=kOutput, calls=%fused_computation.23 | convolution fusion | flops 40278622208 | bytes 22675456 | tf_op jit(solution)/shard_map/dot_general | solution.py:79
  510.8 13.2 %copy.21 = bf16[64,25,2,512]{0,1,2,3:T(8,128)(2,1)} copy(bf16[64,25,2,512]{3,2,1,0:T(2,128)(2,1)S(1)} %convert_element_type.106) | data formatting | bytes 6553600 | tf_op jit(solution)/shard_map/convert_element_type | solution.py:83
  531.8 23.9 %copy.12 = bf16[2,2,64,25,512]{2,3,1,0,4:T(8,128)(2,1)} copy(bf16[2,2,64,25,512]{4,2,3,1,0:T(8,128)(2,1)} %pad_maximum_fusion) | data formatting | bytes 13107200 | tf_op jit(solution)/shard_map/stack | solution.py:84
  555.7 20.9 %fusion = f32[2,64,1,64,512]{1,3,0,4,2:T(8,128)} fusion(bf16[2,2,64,25,512]{2,3,1,0,4:T(8,128)(2,1)} %copy.12, bf16[64,25,2,512]{0,1,2,3:T(8,128)(2,1)} %copy.21), kind=kOutput, calls=%fused_computation.3 | convolution fusion | flops 423624704 | bytes 26607616 | tf_op jit(solution)/shard_map/opisc,pmsc->oimc/dot_general | solution.py:59
  576.6 63.0 %scatter.4 = f32[2,64,5,64,512]{1,3,0,4,2:T(8,128)} pad(f32[2,64,1,64,512]{1,3,0,4,2:T(8,128)} %fusion, f32[]{:T(128)} %constant.126.clone.1), padding=0_0x0_0x0_4x0_0x0_0 | pad | bytes 100663296 | tf_op jit(solution)/shard_map/scatter | solution.py:86
  639.6 298.8 %while.18 = (s32[]{:T(128)}, bf16[2,64,25,512]{3,1,2,0:T(8,128)(2,1)}, f32[2,64,5,64,512]{1,3,0,4,2:T(8,128)}, bf16[2,2,64,25,512]{2,3,1,0,4:T(8,128)(2,1)}, s32[]{:T(128)}, /*index=5*/s32[]{:T(128)}, s32[]{:T(128)}) while((s32[]{:T(128)}, bf16[2,64,25,512]{3,1,2,0:T(8,128)(2,1)}, f32[2,64,5,64,512]{1,3,0,4,2:T(8,128)}, ...), condition=%wide.region_3.4_spmd, body=%wide.region_2.3_spmd.sunk | while | flops 423624704 | bytes 84934808 | solution.py:95
  642.4 36.5 %collective-permute-done = bf16[2,64,25,512]{3,1,2,0:T(8,128)(2,1)S(1)} collective-permute-done((bf16[2,64,25,512]{3,1,2,0:T(8,128)(2,1)}, bf16[2,64,25,512]{3,1,2,0:T(8,128)(2,1)S(1)}, u32[]{:S(2)}, u32[]{:S(2)}) %collective-permute-start) | collective-permute-done | bytes 3276832 | tf_op jit(solution)/shard_map/while/body/eval_jaxpr/ppermute | solution.py:14
  691.3 20.7 %bitcast_dynamic-update-slice_fusion.2 = f32[2,64,5,64,512]{1,3,0,4,2:T(8,128)} fusion(f32[2,64,5,64,512]{1,3,0,4,2:T(8,128)} %get-tuple-element.204, s32[]{:T(128)S(6)} %select_n.82, bf16[2,64,25,512,1]{1,2,0,4,3:T(8,128)(2,1)} %copy.27, bf16[2,2,64,25,512]{2,3,1,0,4:T(8,128)(2,1)} %get-tuple-element.212), kind=kOutput, calls=%fused_computation.clone.1 | convolution fusion | flops 423624704 | bytes 58720260 | tf_op jit(solution)/shard_map/while/body/eval_jaxpr/opisc,pmsc->oimc/dot_general | solution.py:59
  717.2 36.5 %collective-permute-done = bf16[2,64,25,512]{3,1,2,0:T(8,128)(2,1)S(1)} collective-permute-done((bf16[2,64,25,512]{3,1,2,0:T(8,128)(2,1)}, bf16[2,64,25,512]{3,1,2,0:T(8,128)(2,1)S(1)}, u32[]{:S(2)}, u32[]{:S(2)}) %collective-permute-start) | collective-permute-done | bytes 3276832 | tf_op jit(solution)/shard_map/while/body/eval_jaxpr/ppermute | solution.py:14
  753.7 12.5 %copy.27 = bf16[2,64,25,512,1]{1,2,0,4,3:T(8,128)(2,1)} copy(bf16[2,64,25,512,1]{3,1,2,0,4:T(8,128)(2,1)S(1)} %bitcast.67) | data formatting | bytes 6553600 | tf_op jit(solution)/shard_map/while/body/eval_jaxpr/ppermute | solution.py:14
  766.2 20.7 %bitcast_dynamic-update-slice_fusion.2 = f32[2,64,5,64,512]{1,3,0,4,2:T(8,128)} fusion(f32[2,64,5,64,512]{1,3,0,4,2:T(8,128)} %get-tuple-element.204, s32[]{:T(128)S(6)} %select_n.82, bf16[2,64,25,512,1]{1,2,0,4,3:T(8,128)(2,1)} %copy.27, bf16[2,2,64,25,512]{2,3,1,0,4:T(8,128)(2,1)} %get-tuple-element.212), kind=kOutput, calls=%fused_computation.clone.1 | convolution fusion | flops 423624704 | bytes 58720260 | tf_op jit(solution)/shard_map/while/body/eval_jaxpr/opisc,pmsc->oimc/dot_general | solution.py:59
  792.2 36.5 %collective-permute-done = bf16[2,64,25,512]{3,1,2,0:T(8,128)(2,1)S(1)} collective-permute-done((bf16[2,64,25,512]{3,1,2,0:T(8,128)(2,1)}, bf16[2,64,25,512]{3,1,2,0:T(8,128)(2,1)S(1)}, u32[]{:S(2)}, u32[]{:S(2)}) %collective-permute-start) | collective-permute-done | bytes 3276832 | tf_op jit(solution)/shard_map/while/body/eval_jaxpr/ppermute | solution.py:14
  828.7 12.5 %copy.27 = bf16[2,64,25,512,1]{1,2,0,4,3:T(8,128)(2,1)} copy(bf16[2,64,25,512,1]{3,1,2,0,4:T(8,128)(2,1)S(1)} %bitcast.67) | data formatting | bytes 6553600 | tf_op jit(solution)/shard_map/while/body/eval_jaxpr/ppermute | solution.py:14
  841.2 20.6 %bitcast_dynamic-update-slice_fusion.2 = f32[2,64,5,64,512]{1,3,0,4,2:T(8,128)} fusion(f32[2,64,5,64,512]{1,3,0,4,2:T(8,128)} %get-tuple-element.204, s32[]{:T(128)S(6)} %select_n.82, bf16[2,64,25,512,1]{1,2,0,4,3:T(8,128)(2,1)} %copy.27, bf16[2,2,64,25,512]{2,3,1,0,4:T(8,128)(2,1)} %get-tuple-element.212), kind=kOutput, calls=%fused_computation.clone.1 | convolution fusion | flops 423624704 | bytes 58720260 | tf_op jit(solution)/shard_map/while/body/eval_jaxpr/opisc,pmsc->oimc/dot_general | solution.py:59
  867.1 36.5 %collective-permute-done = bf16[2,64,25,512]{3,1,2,0:T(8,128)(2,1)S(1)} collective-permute-done((bf16[2,64,25,512]{3,1,2,0:T(8,128)(2,1)}, bf16[2,64,25,512]{3,1,2,0:T(8,128)(2,1)S(1)}, u32[]{:S(2)}, u32[]{:S(2)}) %collective-permute-start) | collective-permute-done | bytes 3276832 | tf_op jit(solution)/shard_map/while/body/eval_jaxpr/ppermute | solution.py:14
  903.6 12.5 %copy.27 = bf16[2,64,25,512,1]{1,2,0,4,3:T(8,128)(2,1)} copy(bf16[2,64,25,512,1]{3,1,2,0,4:T(8,128)(2,1)S(1)} %bitcast.67) | data formatting | bytes 6553600 | tf_op jit(solution)/shard_map/while/body/eval_jaxpr/ppermute | solution.py:14
  916.0 20.7 %bitcast_dynamic-update-slice_fusion.2 = f32[2,64,5,64,512]{1,3,0,4,2:T(8,128)} fusion(f32[2,64,5,64,512]{1,3,0,4,2:T(8,128)} %get-tuple-element.204, s32[]{:T(128)S(6)} %select_n.82, bf16[2,64,25,512,1]{1,2,0,4,3:T(8,128)(2,1)} %copy.27, bf16[2,2,64,25,512]{2,3,1,0,4:T(8,128)(2,1)} %get-tuple-element.212), kind=kOutput, calls=%fused_computation.clone.1 | convolution fusion | flops 423624704 | bytes 58720260 | tf_op jit(solution)/shard_map/while/body/eval_jaxpr/opisc,pmsc->oimc/dot_general | solution.py:59
  938.3 124.9 %copy.14 = f32[2,64,5,64,512]{4,3,2,1,0:T(8,128)} copy(f32[2,64,5,64,512]{1,3,0,4,2:T(8,128)} %get-tuple-element.127) | data formatting | bytes 167772160 | tf_op jit(solution)/shard_map/while | solution.py:95
  (21 shorter events, 70.3 us)
Async XLA Ops:
  6.5 198.5 %all-gather.2.cloned.1.call-start = ((), (), s32[]{:S(2)}) async-start(), calls=%async_computation | async-start | bytes 26214400 | tf_op jit(solution)/shard_map/all_gather | solution.py:76
  639.6 39.3 %collective-permute-start = (bf16[2,64,25,512]{3,1,2,0:T(8,128)(2,1)}, bf16[2,64,25,512]{3,1,2,0:T(8,128)(2,1)S(1)}, u32[]{:S(2)}, u32[]{:S(2)}) collective-permute-start(bf16[2,64,25,512]{3,1,2,0:T(8,128)(2,1)} %get-tuple-element.203), channel_id=1, source_target_pairs={{0,7},{1,0},{2,1},{3,2},{4,3},{5,4},{6,5},{7,6},{8,15},{9,8},{10,9... | collective-permute-start | bytes 9830408 | tf_op jit(solution)/shard_map/while/body/eval_jaxpr/ppermute | solution.py:14
  713.6 40.1 %collective-permute-start = (bf16[2,64,25,512]{3,1,2,0:T(8,128)(2,1)}, bf16[2,64,25,512]{3,1,2,0:T(8,128)(2,1)S(1)}, u32[]{:S(2)}, u32[]{:S(2)}) collective-permute-start(bf16[2,64,25,512]{3,1,2,0:T(8,128)(2,1)} %get-tuple-element.203), channel_id=1, source_target_pairs={{0,7},{1,0},{2,1},{3,2},{4,3},{5,4},{6,5},{7,6},{8,15},{9,8},{10,9... | collective-permute-start | bytes 9830408 | tf_op jit(solution)/shard_map/while/body/eval_jaxpr/ppermute | solution.py:14
  788.6 40.1 %collective-permute-start = (bf16[2,64,25,512]{3,1,2,0:T(8,128)(2,1)}, bf16[2,64,25,512]{3,1,2,0:T(8,128)(2,1)S(1)}, u32[]{:S(2)}, u32[]{:S(2)}) collective-permute-start(bf16[2,64,25,512]{3,1,2,0:T(8,128)(2,1)} %get-tuple-element.203), channel_id=1, source_target_pairs={{0,7},{1,0},{2,1},{3,2},{4,3},{5,4},{6,5},{7,6},{8,15},{9,8},{10,9... | collective-permute-start | bytes 9830408 | tf_op jit(solution)/shard_map/while/body/eval_jaxpr/ppermute | solution.py:14
  863.5 40.1 %collective-permute-start = (bf16[2,64,25,512]{3,1,2,0:T(8,128)(2,1)}, bf16[2,64,25,512]{3,1,2,0:T(8,128)(2,1)S(1)}, u32[]{:S(2)}, u32[]{:S(2)}) collective-permute-start(bf16[2,64,25,512]{3,1,2,0:T(8,128)(2,1)} %get-tuple-element.203), channel_id=1, source_target_pairs={{0,7},{1,0},{2,1},{3,2},{4,3},{5,4},{6,5},{7,6},{8,15},{9,8},{10,9... | collective-permute-start | bytes 9830408 | tf_op jit(solution)/shard_map/while/body/eval_jaxpr/ppermute | solution.py:14
Sparse Core Ops, SparseCore 0:
  9.2 195.7 all-gather.1
where the time goes:
time: 1080 us; the launch traced here: 1070 us
  local copies, waits for them, and re-layouts  348 us (32%)
  waiting for transfers between devices  325 us (30%)
  other arithmetic  218 us (20%)
  matrix products  152 us (14%)
  between operations  13.7 us (1%)
  starting transfers between devices  13.6 us (1%)
    all_gather x1, waiting for transfers between devices, shards(): whole_series = lax.all_gather(voltages, 'tm', axis=1, tiled=True)  178 us
    ppermute x4, waiting for transfers between devices, from_behind(): return lax.ppermute(value, axis, pairs)  146 us
    add x1, other arithmetic, polyphase(): filtered + taper[tap_index][None, None, :] * frames[:, tap_index:tap_inde...  134 us
    while x1, local copies, waits for them, and re-layouts, shards(): carried_out = lax.fori_loop(1, lag_count, lag_step, (own_block, visibility))  125 us
    dot_general x5, matrix products, correlate(): jnp.einsum('opisc,pmsc->oimc', conjugated, partner_block, preferred_eleme...  104 us
    scatter x1, local copies, waits for them, and re-layouts, shards(): visibility.at[:, :, 0].set(correlate(conjugated, own_block, spectra_count))  63 us
    ppermute x4, local copies, waits for them, and re-layouts, from_behind(): return lax.ppermute(value, axis, pairs)  49.8 us
    dot_general x1, matrix products, shards(): jnp.dot(twisted, table, precision=lax.Precision.HIGHEST, preferred_elemen...  48.6 us
  transfers between devices with their start and end apart: 5, of which 5 were waited for; matrix products, arithmetic and copies ran while one was open for 2% of the time, Pallas kernels for 0%

commit v1 on v0

v1 whole, which is shorter than its diff:
```python
import math

import jax
import jax.numpy as jnp
import numpy as np
from jax import lax
from jax.experimental import pallas as pl
from jax.experimental.pallas import tpu as pltpu
from jax.sharding import PartitionSpec as P

NSPEC = 25
LANES = 128


def from_behind(value, axis, steps):
    count = lax.axis_size(axis)
    pairs = [(source, (source + steps) % count) for source in range(count)]
    return lax.ppermute(value, axis, pairs)


def dft_table(segment, channel_count, frame_len):
    sample_idx = np.arange(segment, dtype=np.int64)[:, None]
    channel_idx = np.arange(channel_count, dtype=np.int64)[None, :]
    angles = 2.0 * math.pi / segment * (sample_idx * channel_idx % segment)
    cosine, sine = np.cos(angles), np.sin(angles)
    upper = np.concatenate([cosine, -sine], axis=1)
    lower = np.concatenate([sine, cosine], axis=1)
    table = np.concatenate([upper, lower], axis=0) / math.sqrt(frame_len)
    return table.astype(np.float32)


def fold_twiddle(filtered, tm_count, frame_len):
    row_count = filtered.shape[0]
    segment = frame_len // tm_count
    pieces = filtered.reshape(row_count, tm_count, segment)
    blocks = []
    for residue in range(tm_count):
        outer = 2.0 * math.pi / tm_count * (residue * np.arange(tm_count) % tm_count)
        inner = 2.0 * math.pi / frame_len * (residue * np.arange(segment) % frame_len)
        inner_cos = np.cos(inner).astype(np.float32)[None, :]
        inner_sin = np.sin(inner).astype(np.float32)[None, :]
        sum_real = sum(float(np.round(np.cos(a), 15)) * pieces[:, n] for n, a in enumerate(outer))
        sum_imag = sum(float(np.round(-np.sin(a), 15)) * pieces[:, n] for n, a in enumerate(outer))
        twisted_real = sum_real * inner_cos + sum_imag * inner_sin
        twisted_imag = sum_imag * inner_cos - sum_real * inner_sin
        blocks.append(jnp.concatenate([twisted_real, twisted_imag], axis=1))
    return jnp.stack(blocks)


def polyphase(series, taper, spectra_count):
    row_count = series.shape[0]
    tap_count, frame_len = taper.shape
    frames = series.reshape(row_count, spectra_count + tap_count - 1, frame_len)
    frames = jnp.transpose(frames, (1, 0, 2))
    filtered = jnp.zeros((spectra_count, row_count, frame_len), jnp.float32)
    for tap_index in range(tap_count):
        filtered = filtered + taper[tap_index][None, None, :] * frames[
            tap_index : tap_index + spectra_count
        ].astype(jnp.float32)
    return filtered


def correlate_kernel(inputs, channels, own_ref, partner_ref, *rest):
    out_ref, products = rest[-2], rest[-1]
    scale = jnp.float32(1.0 / NSPEC)

    def multiply(c, carry):
        products[pl.ds(c * inputs, inputs), :] = (
            jnp.dot(own_ref[c], partner_ref[c], preferred_element_type=jnp.float32) * scale
        )
        return carry

    lax.fori_loop(0, channels, multiply, 0, unroll=8)

    def turn(i, carry):
        tile = jnp.transpose(products[pl.ds(i, channels, stride=inputs), :])
        out_ref[0, i, 0] = tile[:inputs]
        out_ref[1, i, 0] = tile[inputs:]
        return carry

    lax.fori_loop(0, inputs, turn, 0, unroll=4)


def correlate(own, partner, visibility, lag, lag_count):
    channel_count, inputs, depth = own.shape
    block = min(LANES, channel_count)
    out_shape = (2, inputs, lag_count, inputs, channel_count)
    in_specs = [
        pl.BlockSpec((block, inputs, depth), lambda c: (c, 0, 0)),
        pl.BlockSpec((block, depth, 2 * inputs), lambda c: (c, 0, 0)),
    ]
    operands = [own, partner]
    aliases = {}
    if visibility is not None:
        in_specs.append(pl.BlockSpec(memory_space=pl.ANY))
        operands.append(visibility)
        aliases = {2: 0}

    def kernel(*refs):
        correlate_kernel(inputs, block, *refs)

    return pl.pallas_call(
        kernel,
        grid=(channel_count // block,),
        out_shape=jax.ShapeDtypeStruct(out_shape, jnp.float32),
        in_specs=in_specs,
        out_specs=pl.BlockSpec((2, inputs, 1, inputs, block), lambda c: (0, 0, lag, 0, c)),
        scratch_shapes=[pltpu.VMEM((block * inputs, 2 * inputs), jnp.float32)],
        input_output_aliases=aliases,
        compiler_params=pltpu.CompilerParams(vmem_limit_bytes=40 * 1024 * 1024),
        cost_estimate=pl.CostEstimate(
            flops=50_000_000_000, bytes_accessed=32_000_000, transcendentals=0
        ),
    )(*operands)


def pad_depth(value, axis, depth):
    widths = [(0, 0)] * value.ndim
    widths[axis] = (0, depth - value.shape[axis])
    return jnp.pad(value, widths)


def partner_form(block, depth):
    real, imag = block[:, :, 0], block[:, :, 1]
    upper = jnp.concatenate([real, -imag], axis=-1)
    lower = jnp.concatenate([imag, real], axis=-1)
    both = jnp.concatenate([pad_depth(upper, 0, depth), pad_depth(lower, 0, depth)], axis=0)
    return jnp.transpose(both, (1, 0, 2))


def shards(voltages, taper):
    tm_count = lax.axis_size("tm")
    stat_count = lax.axis_size("stat")
    local_inputs = voltages.shape[0]
    frame_len = taper.shape[1]
    segment = frame_len // tm_count
    channel_count = frame_len // 2 // tm_count
    lag_count = stat_count // 2 + 1
    per = local_inputs // tm_count
    depth = 32
    table = dft_table(segment, channel_count, frame_len)

    series = lax.all_to_all(voltages, "tm", split_axis=0, concat_axis=1, tiled=True)
    filtered = polyphase(series, taper, NSPEC)
    twisted = fold_twiddle(filtered.reshape(NSPEC * per, frame_len), tm_count, frame_len)
    spectra = jnp.dot(
        twisted.reshape(tm_count * NSPEC * per, 2 * segment),
        table,
        precision=lax.Precision.HIGH,
        preferred_element_type=jnp.float32,
    ).astype(jnp.bfloat16)
    spectra = spectra.reshape(tm_count, NSPEC * per, 2 * channel_count)
    spectra = lax.all_to_all(spectra, "tm", split_axis=0, concat_axis=0, tiled=True)
    spectra = spectra.reshape(tm_count, NSPEC, per, 2, channel_count)
    block = jnp.transpose(spectra, (1, 4, 3, 0, 2)).reshape(
        NSPEC, channel_count, 2 * local_inputs
    )
    unpacked = block.reshape(NSPEC, channel_count, 2, local_inputs)
    own = jnp.transpose(pad_depth(unpacked, 0, depth), (1, 3, 2, 0)).reshape(
        channel_count, local_inputs, 2 * depth
    )
    visibility = None
    for lag in range(lag_count):
        following = from_behind(block, "stat", -1) if lag < lag_count - 1 else None
        partner = partner_form(
            block.reshape(NSPEC, channel_count, 2, local_inputs), depth
        )
        visibility = correlate(own, partner, visibility, lag, lag_count)
        block = following
    return visibility[None]


def solution(mesh):
    return jax.shard_map(
        shards,
        mesh=mesh,
        in_specs=(P("stat", "tm"), P()),
        out_specs=P("tm", None, "stat", None, None, None),
        check_vma=False,
    )
```

time: 1080 us -> 660 us (0.61)
  waiting for transfers between devices: 325 us -> 75 us
  local copies, waits for them, and re-layouts: 348 us -> 170 us
  Pallas kernels: 0 us -> 139 us
  matrix products: 152 us -> 26.9 us
  blocking collectives: 0 us -> 40.5 us
  other arithmetic: 218 us -> 182 us
  between operations: 13.7 us -> 0.72 us
    all_gather x1 -> x0, waiting for transfers between devices: 178 us -> none  [shards(): whole_series = lax.all_gather(voltages, 'tm', axis=1, tiled=True)]
    pallas_call x0 -> x5, Pallas kernels: none -> 139 us  [correlate(): pl.pallas_call(kernel, grid=(channel_count // block,), out_shape=jax.Shap...]
    while x5 -> x0, local copies, waits for them, and re-layouts: 132 us -> none  [the longest x1 125 us: shards(): carried_out = lax.fori_loop(1, lag_count, lag_step, (own_block, visibility))]
    ppermute x4, waiting for transfers between devices: 146 us -> 15.2 us  [from_behind(): return lax.ppermute(value, axis, pairs)]
    dot_general x6 -> x1, matrix products: 152 us -> 26.9 us  [shards(): jnp.dot(twisted.reshape(tm_count * NSPEC * per, 2 * segment), table, prec...]
    add x1, other arithmetic: 134 us -> 40.6 us  [polyphase(): filtered + taper[tap_index][None, None, :] * frames[tap_index:tap_index +...]
    unnamed x1 -> x46, local copies, waits for them, and re-layouts: 22.7 us -> 89.3 us
    scatter x1 -> x0, local copies, waits for them, and re-layouts: 63 us -> none  [shards(): visibility.at[:, :, 0].set(correlate(conjugated, own_block, spectra_count))]
  transfers between devices with their start and end apart: 5 -> 5, of which waited for: 5 -> 4; matrix products, arithmetic and copies ran while one was open for 2% -> 3% of each run, Pallas kernels for 0% -> 17%
where the time goes in v1:
time: 660 us; the launch traced here: 651 us
  other arithmetic  182 us (28%)
  local copies, waits for them, and re-layouts  170 us (26%)
  Pallas kernels  139 us (21%)
  waiting for transfers between devices  75 us (11%)
  blocking collectives  40.5 us (6%)
  matrix products  26.9 us (4%)
  starting transfers between devices  16.4 us (2%)
    pallas_call x5, Pallas kernels, correlate(): pl.pallas_call(kernel, grid=(channel_count // block,), out_shape=jax.Shap...  139 us
    unnamed x46, local copies, waits for them, and re-layouts  89.3 us
    all_to_all x1, waiting for transfers between devices, shards(): lax.all_to_all(voltages, 'tm', split_axis=0, concat_axis=1, tiled=True)  59.8 us
    concatenate x5, other arithmetic, partner_form(): upper = jnp.concatenate([real, -imag], axis=-1)  58.4 us
    transpose x5, other arithmetic, partner_form(): return jnp.transpose(both, (1, 0, 2))  46.6 us
    add x1, other arithmetic, polyphase(): filtered + taper[tap_index][None, None, :] * frames[tap_index:tap_index +...  40.6 us
    all_to_all x1, blocking collectives, shards(): lax.all_to_all(spectra, 'tm', split_axis=0, concat_axis=0, tiled=True)  40.5 us
    dot_general x1, matrix products, shards(): jnp.dot(twisted.reshape(tm_count * NSPEC * per, 2 * segment), table, prec...  26.9 us
  transfers between devices with their start and end apart: 5, of which 4 were waited for; matrix products, arithmetic and copies ran while one was open for 3% of the time, Pallas kernels for 17%

profile of v1, /device:TPU:0, one launch (start us, length us, event | category | flops | bytes accessed | tf_op | source)
XLA Modules:
  0.0 650.8 jit_solution(5762915165610259702)
XLA Ops:
  5.5 59.8 %all-to-all-done = bf16[4,16,40960]{2,1,0:T(8,128)(2,1)} async-done(((bf16[4,16,40960]{2,1,0:T(8,128)(2,1)}), bf16[4,16,40960]{2,1,0:T(8,128)(2,1)}, u32[]{:S(2)}, u32[]{:S(2)}) %all-to-all-start) | async-done | bytes 5242912 | tf_op jit(solution)/shard_map/all_to_all | solution.py:143
  65.3 8.9 %copy.65 = bf16[16,4,40960]{2,1,0:T(4,128)(2,1)} copy(bf16[16,4,40960]{2,0,1:T(8,128)(2,1)} %bitcast.2) | data formatting | bytes 10485760 | tf_op jit(solution)/shard_map/all_to_all | solution.py:143
  74.2 8.1 %reshape.50 = bf16[16,40,4096]{2,1,0:T(8,128)(2,1)} reshape(bf16[16,4,40960]{2,1,0:T(4,128)(2,1)} %copy.65) | data formatting | bytes 10485760 | tf_op jit(solution)/shard_map/reshape | solution.py:53
  82.3 40.6 %multiply_add_fusion = f32[25,16,4096]{2,0,1:T(8,128)S(1)} fusion(bf16[40,16,4096]{2,0,1:T(8,128)(2,1)} %bitcast.159, f32[4096]{0:T(1024)S(1)} %bitcast.195, f32[4096]{0:T(1024)S(1)} %bitcast.196, f32[4096]{0:T(1024)S(1)} %bitcast.182, f32[4096]{0:T(1024)S(1)} %bitcast.183, f32[4096]{0:T(1024)S(1)} %bitcast.184, f32[4096]{0:T(1024)S(1)} %bitcast.185, ...), kind=kLoop, calls=%fused_computation.27 | loop fusion | flops 77004800 | bytes 59244544 | tf_op jit(solution)/shard_map/add | solution.py:57
  129.5 8.7 %reshape_reshape.7 = f32[400,4,1024]{2,1,0:T(4,128)} reshape(f32[25,16,4096]{2,1,0:T(8,128)} %copy.66) | data formatting | bytes 13107200 | tf_op jit(solution)/shard_map/reshape;reshape | solution.py:35
  138.3 14.9 %fusion.32 = (f32[400,1,1024]{2,1,0:T(1,128)S(1)}, f32[400,1,1024]{2,1,0:T(1,128)S(1)}, f32[400,1,1024]{2,1,0:T(1,128)S(1)}, f32[400,1,1024]{2,1,0:T(1,128)S(1)}) fusion(f32[400,4,1024]{2,1,0:T(4,128)} %reshape_reshape.7), kind=kLoop, calls=%fused_computation.70 | loop fusion | bytes 13107200 | tf_op jit(solution)/shard_map/slice | solution.py:42
  166.6 26.9 %convolution_convert_fusion = bf16[1600,1024]{1,0:T(8,128)(2,1)S(1)} fusion(f32[1600,2048]{1,0:T(8,128)} %bitcast.174, f32[2048,1024]{1,0:T(8,128)S(1)} %bitcast.198), kind=kOutput, calls=%fused_computation.39 | convolution fusion | flops 20134297600 | bytes 24772608 | tf_op jit(solution)/shard_map/dot_general | solution.py:146
  193.5 40.5 %all_to_all.21 = bf16[4,400,1024]{2,1,0:T(8,128)(2,1)S(1)} all-to-all(bf16[4,400,1024]{2,1,0:T(8,128)(2,1)S(1)} %bitcast.180), channel_id=1, replica_groups=mesh['tm'=4,'stat'=8] {'tm'}, dimensions={0} | all-to-all | bytes 6553600 | tf_op jit(solution)/shard_map/all_to_all | solution.py:153
  271.2 13.0 %copy.87.refs_0_ = bf16[512,64,64]{2,1,0:T(8,128)(2,1)} copy(bf16[512,64,64]{0,2,1:T(8,128)(2,1)} %bitcast.173) | data formatting | bytes 8388608 | tf_op jit(solution)/shard_map/reshape | solution.py:159
  285.0 12.3 %fusion.28 = (bf16[32,512,128]{2,0,1:T(8,128)(2,1)}, bf16[32,512,128]{2,0,1:T(8,128)(2,1)}) fusion(bf16[25,512,64]{2,0,1:T(8,128)(2,1)} %bitcast_negate_fusion, bf16[25,512,64]{2,0,1:T(8,128)(2,1)} %bitcast.168, bf16[25,512,64]{2,0,1:T(8,128)(2,1)} %bitcast.160), kind=kLoop, calls=%fused_computation.36 | loop fusion | flops 27262976 | bytes 13303808 | tf_op jit(solution)/shard_map/concatenate | solution.py:125
  297.3 9.3 %maximum_bitcast_fusion.4.refs_1_ = bf16[512,64,128]{2,1,0:T(8,128)(2,1)} fusion(bf16[32,512,128]{2,0,1:T(8,128)(2,1)} %get-tuple-element.26, bf16[32,512,128]{2,0,1:T(8,128)(2,1)} %get-tuple-element.25), kind=kLoop, calls=%fused_computation.26 | loop fusion | flops 16777216 | bytes 16777216 | tf_op jit(solution)/shard_map/transpose | solution.py:128
  309.9 27.7 %shard_map.109.refs_2_ = f32[2,64,5,64,512]{4,3,2,1,0:T(8,128)} custom-call(bf16[512,64,64]{2,1,0:T(8,128)(2,1)S(1)} %copy-done, bf16[512,64,128]{2,1,0:T(8,128)(2,1)} %maximum_bitcast_fusion.4.refs_1_), custom_call_target="tpu_custom_call" | custom-call | flops 49999998976 | bytes 32000000 | tf_op jit(solution)/shard_map/pallas_call | solution.py:102
  358.0 11.6 %fusion.26 = (bf16[32,512,128]{2,0,1:T(8,128)(2,1)}, bf16[32,512,128]{2,0,1:T(8,128)(2,1)}) fusion(bf16[25,512,64]{2,0,1:T(8,128)(2,1)} %bitcast_negate_fusion.1, bf16[25,512,64]{2,0,1:T(8,128)(2,1)} %bitcast.169, bf16[25,512,64]{2,0,1:T(8,128)(2,1)} %bitcast.161), kind=kLoop, calls=%fused_computation.34 | loop fusion | flops 27262976 | bytes 13303808 | tf_op jit(solution)/shard_map/concatenate | solution.py:125
  369.7 9.3 %maximum_bitcast_fusion.3.refs_1_ = bf16[512,64,128]{2,1,0:T(8,128)(2,1)} fusion(bf16[32,512,128]{2,0,1:T(8,128)(2,1)} %get-tuple-element.28, bf16[32,512,128]{2,0,1:T(8,128)(2,1)} %get-tuple-element.27), kind=kLoop, calls=%fused_computation.25 | loop fusion | flops 16777216 | bytes 16777216 | tf_op jit(solution)/shard_map/transpose | solution.py:128
  385.3 27.7 %shard_map.110.refs_2_ = f32[2,64,5,64,512]{4,3,2,1,0:T(8,128)} custom-call(bf16[512,64,64]{2,1,0:T(8,128)(2,1)S(1)} %copy-done.1, bf16[512,64,128]{2,1,0:T(8,128)(2,1)} %maximum_bitcast_fusion.3.refs_1_, f32[2,64,5,64,512]{4,3,2,1,0:T(8,128)} %shard_map.109.refs_2_), custom_call_target="tpu_custom_call", output_to_operand_aliasing={{}: (2, {})} | custom-call | flops 49999998976 | bytes 32000000 | tf_op jit(solution)/shard_map/pallas_call | solution.py:102
  438.5 11.5 %fusion.24 = (bf16[32,512,128]{2,0,1:T(8,128)(2,1)}, bf16[32,512,128]{2,0,1:T(8,128)(2,1)}) fusion(bf16[25,512,64]{2,0,1:T(8,128)(2,1)} %bitcast_negate_fusion.2, bf16[25,512,64]{2,0,1:T(8,128)(2,1)} %bitcast.170, bf16[25,512,64]{2,0,1:T(8,128)(2,1)} %bitcast.162), kind=kLoop, calls=%fused_computation.32 | loop fusion | flops 27262976 | bytes 13303808 | tf_op jit(solution)/shard_map/concatenate | solution.py:125
  450.0 9.4 %maximum_bitcast_fusion.2.refs_1_ = bf16[512,64,128]{2,1,0:T(8,128)(2,1)} fusion(bf16[32,512,128]{2,0,1:T(8,128)(2,1)} %get-tuple-element.30, bf16[32,512,128]{2,0,1:T(8,128)(2,1)} %get-tuple-element.29), kind=kLoop, calls=%fused_computation.24 | loop fusion | flops 16777216 | bytes 16777216 | tf_op jit(solution)/shard_map/transpose | solution.py:128
  466.4 27.9 %shard_map.111.refs_2_ = f32[2,64,5,64,512]{4,3,2,1,0:T(8,128)} custom-call(bf16[512,64,64]{2,1,0:T(8,128)(2,1)S(1)} %copy-done.2, bf16[512,64,128]{2,1,0:T(8,128)(2,1)} %maximum_bitcast_fusion.2.refs_1_, f32[2,64,5,64,512]{4,3,2,1,0:T(8,128)} %shard_map.110.refs_2_), custom_call_target="tpu_custom_call", output_to_operand_aliasing={{}: (2, {})} | custom-call | flops 49999998976 | bytes 32000000 | tf_op jit(solution)/shard_map/pallas_call | solution.py:102
  519.3 11.5 %fusion.22 = (bf16[32,512,128]{2,0,1:T(8,128)(2,1)}, bf16[32,512,128]{2,0,1:T(8,128)(2,1)}) fusion(bf16[25,512,64]{2,0,1:T(8,128)(2,1)} %bitcast_negate_fusion.3, bf16[25,512,64]{2,0,1:T(8,128)(2,1)} %bitcast.171, bf16[25,512,64]{2,0,1:T(8,128)(2,1)} %bitcast.163), kind=kLoop, calls=%fused_computation.30 | loop fusion | flops 27262976 | bytes 13303808 | tf_op jit(solution)/shard_map/concatenate | solution.py:125
  530.8 9.4 %maximum_bitcast_fusion.1.refs_1_ = bf16[512,64,128]{2,1,0:T(8,128)(2,1)} fusion(bf16[32,512,128]{2,0,1:T(8,128)(2,1)} %get-tuple-element.32, bf16[32,512,128]{2,0,1:T(8,128)(2,1)} %get-tuple-element.31), kind=kLoop, calls=%fused_computation.23 | loop fusion | flops 16777216 | bytes 16777216 | tf_op jit(solution)/shard_map/transpose | solution.py:128
  547.3 27.9 %shard_map.112.refs_2_ = f32[2,64,5,64,512]{4,3,2,1,0:T(8,128)} custom-call(bf16[512,64,64]{2,1,0:T(8,128)(2,1)S(1)} %copy-done.3, bf16[512,64,128]{2,1,0:T(8,128)(2,1)} %maximum_bitcast_fusion.1.refs_1_, f32[2,64,5,64,512]{4,3,2,1,0:T(8,128)} %shard_map.111.refs_2_), custom_call_target="tpu_custom_call", output_to_operand_aliasing={{}: (2, {})} | custom-call | flops 49999998976 | bytes 32000000 | tf_op jit(solution)/shard_map/pallas_call | solution.py:102
  598.5 11.5 %fusion.20 = (bf16[32,512,128]{2,0,1:T(8,128)(2,1)}, bf16[32,512,128]{2,0,1:T(8,128)(2,1)}) fusion(bf16[25,512,64]{2,0,1:T(8,128)(2,1)} %bitcast_negate_fusion.4, bf16[25,512,64]{2,0,1:T(8,128)(2,1)} %bitcast.172, bf16[25,512,64]{2,0,1:T(8,128)(2,1)} %bitcast.164), kind=kLoop, calls=%fused_computation.28 | loop fusion | flops 27262976 | bytes 13303808 | tf_op jit(solution)/shard_map/concatenate | solution.py:125
  610.0 9.3 %maximum_bitcast_fusion.refs_1_ = bf16[512,64,128]{2,1,0:T(8,128)(2,1)} fusion(bf16[32,512,128]{2,0,1:T(8,128)(2,1)} %get-tuple-element.34, bf16[32,512,128]{2,0,1:T(8,128)(2,1)} %get-tuple-element.33), kind=kLoop, calls=%fused_computation.22 | loop fusion | flops 16777216 | bytes 16777216 | tf_op jit(solution)/shard_map/transpose | solution.py:128
  622.6 27.7 %shard_map.113 = f32[2,64,5,64,512]{4,3,2,1,0:T(8,128)} custom-call(bf16[512,64,64]{2,1,0:T(8,128)(2,1)S(1)} %copy-done.4, bf16[512,64,128]{2,1,0:T(8,128)(2,1)} %maximum_bitcast_fusion.refs_1_, f32[2,64,5,64,512]{4,3,2,1,0:T(8,128)} %shard_map.112.refs_2_), custom_call_target="tpu_custom_call", output_to_operand_aliasing={{}: (2, {})} | custom-call | flops 49999998976 | bytes 32000000 | tf_op jit(solution)/shard_map/pallas_call | solution.py:102
  (80 shorter events, 184.7 us)
Async XLA Ops:
  0.0 5.3 copy-start.9
  0.0 65.3 %all-to-all-start = ((bf16[4,16,40960]{2,1,0:T(8,128)(2,1)}), bf16[4,16,40960]{2,1,0:T(8,128)(2,1)}, u32[]{:S(2)}, u32[]{:S(2)}) async-start(bf16[4,16,40960]{2,1,0:T(8,128)(2,1)} %bitcast.176), calls=%async_computation | async-start | bytes 10485760 | tf_op jit(solution)/shard_map/all_to_all | solution.py:143
  153.2 1.8 copy-start.10
  153.2 1.7 copy-start.11
  153.2 1.7 copy-start.12
  153.2 1.7 copy-start.13
  153.2 1.7 copy-start.14
  153.3 1.7 copy-start.15
  159.8 6.8 %slice-start = ((s8[8388608]{0:T(1024)(128)(4,1)}), s8[4194304]{0:T(1024)(128)(4,1)S(1)}, s32[]{:S(2)}) async-start(s8[8388608]{0:T(1024)(128)(4,1)} %bitcast.197), calls=%async_computation.2 | async-start | bytes 8388608
  160.7 5.9 slice-start.1
  284.2 53.4 %collective-permute-start = (bf16[25,512,128]{1,2,0:T(8,128)(2,1)S(1)}, bf16[25,512,128]{1,2,0:T(8,128)(2,1)}, u32[]{:S(2)}, u32[]{:S(2)}) collective-permute-start(bf16[25,512,128]{1,2,0:T(8,128)(2,1)S(1)} %bitcast.167), channel_id=1, source_target_pairs={{0,7},{1,0},{2,1},{3,2},{4,3},{5,4},{6,5},{7,6},{8,15},{9,8},{10,9... | collective-permute-start | bytes 9830408 | tf_op jit(solution)/shard_map/ppermute | solution.py:18
  306.6 3.4 copy-start
  378.9 39.5 %collective-permute-start.1 = (bf16[25,512,128]{1,2,0:T(8,128)(2,1)}, bf16[25,512,128]{1,2,0:T(8,128)(2,1)S(1)}, u32[]{:S(2)}, u32[]{:S(2)}) collective-permute-start(bf16[25,512,128]{1,2,0:T(8,128)(2,1)} %collective-permute-done), channel_id=1, source_target_pairs={{0,7},{1,0},{2,1},{3,2},{4,3},{5,4},{6,5},{7,6},{8,15},{9,8},{10,9... | collective-permute-start | bytes 9830408 | tf_op jit(solution)/shard_map/ppermute | solution.py:18
  381.9 3.4 copy-start.1
  418.4 1.7 copy-start.5
  450.0 9.4 %copy-start.6 = (bf16[25,512,128]{1,2,0:T(8,128)(2,1)S(1)}, bf16[25,512,128]{1,2,0:T(8,128)(2,1)}, u32[]{:S(2)}) copy-start(bf16[25,512,128]{1,2,0:T(8,128)(2,1)} %copy-done.5) | copy-start | bytes 9830404
  459.4 39.8 %collective-permute-start.2 = (bf16[25,512,128]{1,2,0:T(8,128)(2,1)S(1)}, bf16[25,512,128]{1,2,0:T(8,128)(2,1)S(1)}, u32[]{:S(2)}, u32[]{:S(2)}) collective-permute-start(bf16[25,512,128]{1,2,0:T(8,128)(2,1)S(1)} %copy-done.6), channel_id=1, source_target_pairs={{0,7},{1,0},{2,1},{3,2},{4,3},{5,4},{6,5},{7,6},{8,15},{9,8},{10,9... | collective-permute-start | bytes 9830408 | tf_op jit(solution)/shard_map/ppermute | solution.py:18
  463.0 3.4 copy-start.2
  499.2 1.7 copy-start.7
  530.8 9.4 %copy-start.8 = (bf16[25,512,128]{1,2,0:T(8,128)(2,1)S(1)}, bf16[25,512,128]{1,2,0:T(8,128)(2,1)}, u32[]{:S(2)}) copy-start(bf16[25,512,128]{1,2,0:T(8,128)(2,1)} %copy-done.7) | copy-start | bytes 9830404
  540.2 39.9 %collective-permute-start.3 = (bf16[25,512,128]{1,2,0:T(8,128)(2,1)S(1)}, bf16[25,512,128]{1,2,0:T(8,128)(2,1)S(1)}, u32[]{:S(2)}, u32[]{:S(2)}) collective-permute-start(bf16[25,512,128]{1,2,0:T(8,128)(2,1)S(1)} %copy-done.8), channel_id=1, source_target_pairs={{0,7},{1,0},{2,1},{3,2},{4,3},{5,4},{6,5},{7,6},{8,15},{9,8},{10,9... | collective-permute-start | bytes 9830408 | tf_op jit(solution)/shard_map/ppermute | solution.py:18
  543.9 3.4 copy-start.3
  619.3 3.4 copy-start.4

commit v2 on v1

v2 whole, which is shorter than its diff:
```python
import math

import jax
import jax.numpy as jnp
import numpy as np
from jax import lax
from jax.experimental import pallas as pl
from jax.experimental.pallas import tpu as pltpu
from jax.sharding import PartitionSpec as P

NSPEC = 25
LANES = 128
DEPTH = 32


def from_behind(value, axis, steps):
    count = lax.axis_size(axis)
    pairs = [(source, (source + steps) % count) for source in range(count)]
    return lax.ppermute(value, axis, pairs)


def dft_table(segment, channel_count, frame_len, width):
    sample_idx = np.arange(segment, dtype=np.int64)[:, None]
    channel_idx = np.arange(channel_count, dtype=np.int64)[None, :]
    angles = 2.0 * math.pi / segment * (sample_idx * channel_idx % segment)
    cosine, sine = np.cos(angles), np.sin(angles)
    upper = np.concatenate([cosine, -sine], axis=1)
    lower = np.concatenate([sine, cosine], axis=1)
    table = np.stack([upper, lower]) / math.sqrt(frame_len)
    table = table.reshape(2, segment // width, width, 2 * channel_count)
    return table.transpose(1, 0, 2, 3).reshape(2 * segment, 2 * channel_count).astype(np.float32)


def twiddle_tables(tm_count, frame_len):
    segment = frame_len // tm_count
    turns = np.arange(tm_count)[:, None] * np.arange(segment)[None, :] % frame_len
    angles = 2.0 * math.pi / frame_len * turns
    return np.cos(angles).astype(np.float32), np.sin(angles).astype(np.float32)


def weighted(pieces, weights):
    total = None
    for piece, weight in zip(pieces, weights):
        weight = float(np.round(weight, 15))
        if weight == 0.0:
            continue
        term = piece if weight == 1.0 else (-piece if weight == -1.0 else piece * weight)
        total = term if total is None else total + term
    return jnp.zeros_like(pieces[0]) if total is None else total


def channelize_kernel(tm_count, width, series_ref, taper_ref, cos_ref, sin_ref, out_ref, frames):
    tap_count, frame_len = taper_ref.shape
    segment = frame_len // tm_count
    per_source = series_ref.shape[2] // frame_len
    start = pl.program_id(0) * width
    for source in range(tm_count):
        for frame in range(per_source):
            for outer in range(tm_count):
                column = pl.multiple_of(frame * frame_len + outer * segment + start, width)
                frames[source * per_source + frame, outer] = series_ref[
                    source, :, pl.ds(column, width)
                ].astype(jnp.float32)

    def spectrum(s, carry):
        pieces = []
        for outer in range(tm_count):
            column = pl.multiple_of(outer * segment + start, width)
            total = None
            for tap in range(tap_count):
                term = taper_ref[tap : tap + 1, pl.ds(column, width)] * frames[s + tap, outer]
                total = term if total is None else total + term
            pieces.append(total)
        for residue in range(tm_count):
            angles = 2.0 * math.pi / tm_count * (residue * np.arange(tm_count) % tm_count)
            sum_real = weighted(pieces, np.cos(angles))
            sum_imag = weighted(pieces, -np.sin(angles))
            inner_cos = cos_ref[residue : residue + 1, :]
            inner_sin = sin_ref[residue : residue + 1, :]
            out_ref[residue, s, :, :width] = sum_real * inner_cos + sum_imag * inner_sin
            out_ref[residue, s, :, width:] = sum_imag * inner_cos - sum_real * inner_sin
        return carry

    lax.fori_loop(0, NSPEC, spectrum, 0)


def channelize(series, taper, width):
    tm_count, inputs, samples = series.shape
    tap_count, frame_len = taper.shape
    segment = frame_len // tm_count
    inner_cos, inner_sin = twiddle_tables(tm_count, frame_len)
    frame_count = tm_count * samples // frame_len

    def kernel(*refs):
        channelize_kernel(tm_count, width, *refs)

    return pl.pallas_call(
        kernel,
        grid=(segment // width,),
        out_shape=jax.ShapeDtypeStruct((tm_count, NSPEC, inputs, 2 * segment), jnp.float32),
        in_specs=[
            pl.BlockSpec(series.shape, lambda n: (0, 0, 0)),
            pl.BlockSpec(taper.shape, lambda n: (0, 0)),
            pl.BlockSpec((tm_count, width), lambda n: (0, n)),
            pl.BlockSpec((tm_count, width), lambda n: (0, n)),
        ],
        out_specs=pl.BlockSpec((tm_count, NSPEC, inputs, 2 * width), lambda n: (0, 0, 0, n)),
        scratch_shapes=[pltpu.VMEM((frame_count, tm_count, inputs, width), jnp.float32)],
        compiler_params=pltpu.CompilerParams(vmem_limit_bytes=40 * 1024 * 1024),
        cost_estimate=pl.CostEstimate(
            flops=200_000_000, bytes_accessed=20_000_000, transcendentals=0
        ),
    )(series, taper, inner_cos, inner_sin)


def correlate_kernel(inputs, channels, first, *refs):
    if first:
        partner_ref, out_ref, own_ref, rows, products = refs
    else:
        own_ref, partner_ref, _, out_ref, rows, products = refs
    scale = jnp.float32(1.0 / NSPEC)
    lanes = 2 * inputs
    total = channels * NSPEC
    rows[pl.ds(0, total), :] = partner_ref[...].astype(jnp.float32)
    rows[pl.ds(total, 8), :] = jnp.zeros((8, lanes), jnp.float32)
    lane = lax.broadcasted_iota(jnp.int32, (DEPTH, lanes), 1)
    sign = jnp.where(lane < inputs, 1.0, -1.0).astype(jnp.float32)
    held = lax.broadcasted_iota(jnp.int32, (DEPTH, lanes), 0) < NSPEC

    def multiply(c, carry):
        both = rows[pl.ds(c * NSPEC, DEPTH), :]
        if lanes == LANES:
            swapped = pltpu.roll(both, inputs, 1)
        else:
            swapped = jnp.concatenate([both[:, inputs:], both[:, :inputs]], axis=1)
        right = jnp.concatenate([both * sign, swapped], axis=0).astype(jnp.bfloat16)
        if first:
            turned = jnp.transpose(jnp.where(held, both, 0.0))
            left = jnp.concatenate([turned[:inputs], turned[inputs:]], axis=1)
            left = left.astype(jnp.bfloat16)
            own_ref[c] = left
        else:
            left = own_ref[c]
        products[pl.ds(c * inputs, inputs), :] = (
            jnp.dot(left, right, preferred_element_type=jnp.float32) * scale
        )
        return carry

    lax.fori_loop(0, channels, multiply, 0, unroll=8)

    def turn(i, carry):
        tile = jnp.transpose(products[pl.ds(i, channels, stride=inputs), :])
        out_ref[0, i, 0] = tile[:inputs]
        out_ref[1, i, 0] = tile[inputs:]
        return carry

    lax.fori_loop(0, inputs, turn, 0, unroll=4)


def correlate(own, partner, visibility, lag, lag_count, inputs, channel_count):
    block = min(LANES, channel_count)
    out_shape = [
        jax.ShapeDtypeStruct((2, inputs, lag_count, inputs, channel_count), jnp.float32)
    ]
    out_specs = [pl.BlockSpec((2, inputs, 1, inputs, block), lambda c: (0, 0, lag, 0, c))]
    own_spec = pl.BlockSpec((block, inputs, 2 * DEPTH), lambda c: (c, 0, 0))
    partner_spec = pl.BlockSpec((block * NSPEC, 2 * inputs), lambda c: (c, 0))
    first = own is None
    if first:
        in_specs, operands, aliases = [partner_spec], [partner], {}
        out_shape.append(
            jax.ShapeDtypeStruct((channel_count, inputs, 2 * DEPTH), jnp.bfloat16)
        )
        out_specs.append(own_spec)
    else:
        in_specs = [own_spec, partner_spec, pl.BlockSpec(memory_space=pl.ANY)]
        operands, aliases = [own, partner, visibility], {2: 0}

    def kernel(*refs):
        correlate_kernel(inputs, block, first, *refs)

    results = pl.pallas_call(
        kernel,
        grid=(channel_count // block,),
        out_shape=out_shape,
        in_specs=in_specs,
        out_specs=out_specs,
        scratch_shapes=[
            pltpu.VMEM((block * NSPEC + 8, 2 * inputs), jnp.float32),
            pltpu.VMEM((block * inputs, 2 * inputs), jnp.float32),
        ],
        input_output_aliases=aliases,
        compiler_params=pltpu.CompilerParams(vmem_limit_bytes=40 * 1024 * 1024),
        cost_estimate=pl.CostEstimate(
            flops=35_000_000_000, bytes_accessed=24_000_000, transcendentals=0
        ),
    )(*operands)
    return (results[0], results[1]) if first else (results[0], own)


def shards(voltages, taper):
    tm_count = lax.axis_size("tm")
    stat_count = lax.axis_size("stat")
    local_inputs, samples = voltages.shape
    frame_len = taper.shape[1]
    segment = frame_len // tm_count
    channel_count = frame_len // 2 // tm_count
    lag_count = stat_count // 2 + 1
    per = local_inputs // tm_count
    table = dft_table(segment, channel_count, frame_len, LANES)

    series = lax.all_to_all(
        voltages.reshape(tm_count, per, samples), "tm", split_axis=0, concat_axis=0, tiled=True
    )
    twisted = channelize(series, taper, LANES)
    spectra = jnp.dot(
        twisted.reshape(tm_count * NSPEC * per, 2 * segment),
        table,
        precision=lax.Precision.HIGH,
        preferred_element_type=jnp.float32,
    ).astype(jnp.bfloat16)
    spectra = spectra.reshape(tm_count, NSPEC * per, 2 * channel_count)
    spectra = lax.all_to_all(spectra, "tm", split_axis=0, concat_axis=0, tiled=True)
    spectra = spectra.reshape(tm_count, NSPEC, per, 2, channel_count)
    block = jnp.transpose(spectra, (4, 1, 3, 0, 2)).reshape(
        channel_count * NSPEC, 2 * local_inputs
    )
    visibility = own = None
    for lag in range(lag_count):
        following = from_behind(block, "stat", -1) if lag < lag_count - 1 else None
        visibility, own = correlate(
            own, block, visibility, lag, lag_count, local_inputs, channel_count
        )
        block = following
    return visibility[None]


def solution(mesh):
    return jax.shard_map(
        shards,
        mesh=mesh,
        in_specs=(P("stat", "tm"), P()),
        out_specs=P("tm", None, "stat", None, None, None),
        check_vma=False,
    )
```

time: 660 us -> 393 us (0.60); the launches traced: 651 us -> 392 us
  other arithmetic: 182 us -> 0.01 us
  local copies, waits for them, and re-layouts: 170 us -> 48.4 us
  blocking collectives: 40.5 us -> 105 us
  waiting for transfers between devices: 75 us -> 15.8 us
  Pallas kernels: 139 us -> 186 us
    unnamed x46 -> x10, local copies, waits for them, and re-layouts: 89.3 us -> 0.02 us
    all_to_all x0 -> x1, blocking collectives: none -> 64.8 us  [shards(): lax.all_to_all(voltages.reshape(tm_count, per, samples), 'tm', split_axis...]
    all_to_all x1 -> x0, waiting for transfers between devices: 59.8 us -> none  [shards(): lax.all_to_all(voltages, 'tm', split_axis=0, concat_axis=1, tiled=True)]
    concatenate x5 -> x0, other arithmetic: 58.4 us -> none  [partner_form(): upper = jnp.concatenate([real, -imag], axis=-1)]
    pallas_call x5 -> x6, Pallas kernels: 139 us -> 186 us  [the longest x5 169 us: correlate(): pl.pallas_call(kernel, grid=(channel_count // block,), out_shape=out_shap...]
    transpose x5 -> x0, other arithmetic: 46.6 us -> none  [partner_form(): return jnp.transpose(both, (1, 0, 2))]
    add x3 -> x0, other arithmetic: 45.1 us -> none  [the longest x1 40.6 us: polyphase(): filtered + taper[tap_index][None, None, :] * frames[tap_index:tap_index +...]
    neg x5 -> x0, other arithmetic: 23.3 us -> none  [partner_form(): upper = jnp.concatenate([real, -imag], axis=-1)]
  transfers between devices with their start and end apart: 5 -> 4, of which waited for: 4 -> 3; matrix products, arithmetic and copies ran while one was open for 3% -> 0% of each run, Pallas kernels for 17% -> 35%
where the time goes in v2:
time: 393 us; the launch traced here: 392 us
  Pallas kernels  186 us (47%)
  blocking collectives  105 us (27%)
  local copies, waits for them, and re-layouts  48.4 us (12%)
  matrix products  24.9 us (6%)
  waiting for transfers between devices  15.8 us (4%)
  starting transfers between devices  11.5 us (3%)
    pallas_call x5, Pallas kernels, correlate(): pl.pallas_call(kernel, grid=(channel_count // block,), out_shape=out_shap...  169 us
    all_to_all x1, blocking collectives, shards(): lax.all_to_all(voltages.reshape(tm_count, per, samples), 'tm', split_axis...  64.8 us
    all_to_all x1, blocking collectives, shards(): lax.all_to_all(spectra, 'tm', split_axis=0, concat_axis=0, tiled=True)  40.1 us
    reshape x2, local copies, waits for them, and re-layouts, shards(): jnp.transpose(spectra, (4, 1, 3, 0, 2))  25.7 us
    dot_general x1, matrix products, shards(): jnp.dot(twisted.reshape(tm_count * NSPEC * per, 2 * segment), table, prec...  24.9 us
    pallas_call x1, Pallas kernels, channelize(): pl.pallas_call(kernel, grid=(segment // width,), out_shape=jax.ShapeDtype...  16.9 us
    ppermute x4, waiting for transfers between devices, from_behind(): return lax.ppermute(value, axis, pairs)  15.8 us
    transpose x1, local copies, waits for them, and re-layouts, shards(): jnp.transpose(spectra, (4, 1, 3, 0, 2))  15.3 us
  transfers between devices with their start and end apart: 4, of which 3 were waited for; matrix products, arithmetic and copies ran while one was open for 0% of the time, Pallas kernels for 35%

profile of v2, /device:TPU:0, one launch (start us, length us, event | category | flops | bytes accessed | tf_op | source)
XLA Modules:
  0.0 391.8 jit_solution(5882743661029700158)
XLA Ops:
  0.0 64.8 %all_to_all.10.refs_0_ = bf16[4,16,40960]{2,1,0:T(8,128)(2,1)S(1)} all-to-all(bf16[4,16,40960]{2,1,0:T(8,128)(2,1)} %bitcast.13), channel_id=1, replica_groups=mesh['tm'=4,'stat'=8] {'tm'}, dimensions={0} | all-to-all | bytes 10485760 | tf_op jit(solution)/shard_map/all_to_all | solution.py:212
  64.8 0.0 copy-done.1
  64.8 0.0 copy-done.2
  64.8 0.0 slice-start.1
  64.8 16.9 %shard_map.55 = f32[4,25,16,2048]{3,2,1,0:T(8,128)} custom-call(bf16[4,16,40960]{2,1,0:T(8,128)(2,1)S(1)} %all_to_all.10.refs_0_, f32[16,4096]{1,0:T(8,128)S(1)} %copy-done, f32[4,1024]{1,0:T(4,128)S(1)} %copy-done.1, f32[4,1024]{1,0:T(4,128)S(1)} %copy-done.2), custom_call_target="tpu_custom_call" | custom-call | flops 200000000 | bytes 20000000 | tf_op jit(solution)/shard_map/pallas_call | solution.py:97
  81.7 24.9 %convolution_convert_fusion = bf16[1600,1024]{1,0:T(8,128)(2,1)S(1)} fusion(f32[1600,2048]{1,0:T(8,128)} %bitcast.12, f32[2048,1024]{1,0:T(8,128)S(1)} %bitcast.16), kind=kOutput, calls=%fused_computation | convolution fusion | flops 20134297600 | bytes 24772608 | tf_op jit(solution)/shard_map/dot_general | solution.py:216
  106.6 40.1 %all_to_all.11 = bf16[4,400,1024]{2,1,0:T(8,128)(2,1)} all-to-all(bf16[4,400,1024]{2,1,0:T(8,128)(2,1)S(1)} %bitcast.14), channel_id=1, replica_groups=mesh['tm'=4,'stat'=8] {'tm'}, dimensions={0} | all-to-all | bytes 6553600 | tf_op jit(solution)/shard_map/all_to_all | solution.py:223
  146.7 7.4 %reshape.18 = bf16[4,25,16,2,512]{4,3,2,1,0:T(2,128)(2,1)S(1)} reshape(bf16[4,400,1024]{2,1,0:T(8,128)(2,1)} %all_to_all.11) | data formatting | bytes 6553600 | tf_op jit(solution)/shard_map/reshape | solution.py:224
  154.1 15.3 %copy.10 = bf16[512,25,2,4,16]{1,0,4,3,2:T(8,128)(2,1)} copy(bf16[512,25,2,4,16]{0,2,4,1,3:T(2,128)(2,1)S(1)} %bitcast.11) | data formatting | bytes 6553600 | tf_op jit(solution)/shard_map/transpose | solution.py:225
  169.4 21.4 %reshape.19 = bf16[12800,128]{0,1:T(8,128)(2,1)} reshape(bf16[512,25,2,4,16]{1,0,4,3,2:T(8,128)(2,1)} %copy.10) | data formatting | bytes 6553600 | tf_op jit(solution)/shard_map/reshape | solution.py:225
  190.8 4.3 %copy.11.refs_0_ = bf16[12800,128]{1,0:T(8,128)(2,1)S(1)} copy(bf16[12800,128]{0,1:T(8,128)(2,1)} %reshape.19) | data formatting | bytes 6553600 | tf_op jit(solution)/shard_map/reshape | solution.py:225
  195.1 0.5 collective-permute-start
  195.6 45.7 %shard_map.56 = (f32[2,64,5,64,512]{4,3,2,1,0:T(8,128)}, bf16[512,64,64]{2,1,0:T(8,128)(2,1)S(1)}) custom-call(bf16[12800,128]{1,0:T(8,128)(2,1)S(1)} %copy.11.refs_0_), custom_call_target="tpu_custom_call" | custom-call | flops 35000000512 | bytes 24000000 | tf_op jit(solution)/shard_map/pallas_call | solution.py:182
  241.3 0.0 collective-permute-done.refs_1_
  241.3 3.6 collective-permute-start.1
  244.9 30.9 %shard_map.57.refs_2_ = f32[2,64,5,64,512]{4,3,2,1,0:T(8,128)} custom-call(bf16[512,64,64]{2,1,0:T(8,128)(2,1)S(1)} %get-tuple-element.7.refs_0_, bf16[12800,128]{1,0:T(8,128)(2,1)S(1)} %collective-permute-done.refs_1_, f32[2,64,5,64,512]{4,3,2,1,0:T(8,128)} %get-tuple-element.8.refs_2_), custom_call_target="tpu_custom_call", output_to_operand_aliasing={{}: (2, {})} | custom-call | flops 35000000512 | bytes 24000000 | tf_op jit(solution)/shard_map/pallas_call | solution.py:182
  275.8 5.3 %collective-permute-done.1.refs_1_ = bf16[12800,128]{1,0:T(8,128)(2,1)S(1)} collective-permute-done((bf16[12800,128]{1,0:T(8,128)(2,1)S(1)}, bf16[12800,128]{1,0:T(8,128)(2,1)S(1)}, u32[]{:S(2)}, u32[]{:S(2)}) %collective-permute-start.1) | collective-permute-done | bytes 3276832 | tf_op jit(solution)/shard_map/ppermute | solution.py:19
  281.1 3.7 collective-permute-start.2
  284.8 30.9 %shard_map.58.refs_2_ = f32[2,64,5,64,512]{4,3,2,1,0:T(8,128)} custom-call(bf16[512,64,64]{2,1,0:T(8,128)(2,1)S(1)} %get-tuple-element.7.refs_0_, bf16[12800,128]{1,0:T(8,128)(2,1)S(1)} %collective-permute-done.1.refs_1_, f32[2,64,5,64,512]{4,3,2,1,0:T(8,128)} %shard_map.57.refs_2_), custom_call_target="tpu_custom_call", output_to_operand_aliasing={{}: (2, {})} | custom-call | flops 35000000512 | bytes 24000000 | tf_op jit(solution)/shard_map/pallas_call | solution.py:182
  315.7 5.3 %collective-permute-done.2.refs_1_ = bf16[12800,128]{1,0:T(8,128)(2,1)S(1)} collective-permute-done((bf16[12800,128]{1,0:T(8,128)(2,1)S(1)}, bf16[12800,128]{1,0:T(8,128)(2,1)S(1)}, u32[]{:S(2)}, u32[]{:S(2)}) %collective-permute-start.2) | collective-permute-done | bytes 3276832 | tf_op jit(solution)/shard_map/ppermute | solution.py:19
  321.0 3.7 collective-permute-start.3
  324.7 30.9 %shard_map.59.refs_2_ = f32[2,64,5,64,512]{4,3,2,1,0:T(8,128)} custom-call(bf16[512,64,64]{2,1,0:T(8,128)(2,1)S(1)} %get-tuple-element.7.refs_0_, bf16[12800,128]{1,0:T(8,128)(2,1)S(1)} %collective-permute-done.2.refs_1_, f32[2,64,5,64,512]{4,3,2,1,0:T(8,128)} %shard_map.58.refs_2_), custom_call_target="tpu_custom_call", output_to_operand_aliasing={{}: (2, {})} | custom-call | flops 35000000512 | bytes 24000000 | tf_op jit(solution)/shard_map/pallas_call | solution.py:182
  355.6 5.3 %collective-permute-done.3.refs_1_ = bf16[12800,128]{1,0:T(8,128)(2,1)S(1)} collective-permute-done((bf16[12800,128]{1,0:T(8,128)(2,1)S(1)}, bf16[12800,128]{1,0:T(8,128)(2,1)S(1)}, u32[]{:S(2)}, u32[]{:S(2)}) %collective-permute-start.3) | collective-permute-done | bytes 3276832 | tf_op jit(solution)/shard_map/ppermute | solution.py:19
  360.9 30.9 %shard_map.60 = f32[2,64,5,64,512]{4,3,2,1,0:T(8,128)} custom-call(bf16[512,64,64]{2,1,0:T(8,128)(2,1)S(1)} %get-tuple-element.7.refs_0_, bf16[12800,128]{1,0:T(8,128)(2,1)S(1)} %collective-permute-done.3.refs_1_, f32[2,64,5,64,512]{4,3,2,1,0:T(8,128)} %shard_map.59.refs_2_), custom_call_target="tpu_custom_call", output_to_operand_aliasing={{}: (2, {})} | custom-call | flops 35000000512 | bytes 24000000 | tf_op jit(solution)/shard_map/pallas_call | solution.py:182
  (8 shorter events, 0.0 us)
Async XLA Ops:
  0.0 64.8 %copy-start.1 = (f32[4,1024]{1,0:T(4,128)S(1)}, f32[4,1024]{1,0:T(4,128)}, u32[]{:S(2)}) copy-start(f32[4,1024]{1,0:T(4,128)} %constant.6.clone.refs_2_) | copy-start | bytes 49156
  0.0 64.8 %copy-start.2 = (f32[4,1024]{1,0:T(4,128)S(1)}, f32[4,1024]{1,0:T(4,128)}, u32[]{:S(2)}) copy-start(f32[4,1024]{1,0:T(4,128)} %constant.7.clone.refs_3_) | copy-start | bytes 49156
  0.0 64.8 %copy-start = (f32[16,4096]{1,0:T(8,128)S(1)}, f32[16,4096]{1,0:T(8,128)}, u32[]{:S(2)}) copy-start(f32[16,4096]{1,0:T(8,128)} %refs_1_.1) | copy-start | bytes 786436
  0.0 81.7 %slice-start = ((s8[8388608]{0:T(1024)(128)(4,1)}), s8[4194304]{0:T(1024)(128)(4,1)S(1)}, s32[]{:S(2)}) async-start(s8[8388608]{0:T(1024)(128)(4,1)} %bitcast.15), calls=%async_computation.2 | async-start | bytes 8388608
  64.8 16.9 %slice-start.1 = ((s8[8388608]{0:T(1024)(128)(4,1)}), s8[4194304]{0:T(1024)(128)(4,1)S(1)}, s32[]{:S(2)}) async-start(s8[8388608]{0:T(1024)(128)(4,1)} %bitcast.15), calls=%async_computation.3 | async-start | bytes 8388608
  195.1 46.3 %collective-permute-start = (bf16[12800,128]{1,0:T(8,128)(2,1)S(1)}, bf16[12800,128]{1,0:T(8,128)(2,1)S(1)}, u32[]{:S(2)}, u32[]{:S(2)}) collective-permute-start(bf16[12800,128]{1,0:T(8,128)(2,1)S(1)} %copy.11.refs_0_), channel_id=1, source_target_pairs={{0,7},{1,0},{2,1},{3,2},{4,3},{5,4},{6,5},{7,6},{8,15},{9,8},{10,9... | collective-permute-start | bytes 9830408 | tf_op jit(solution)/shard_map/ppermute | solution.py:19
  241.3 39.8 %collective-permute-start.1 = (bf16[12800,128]{1,0:T(8,128)(2,1)S(1)}, bf16[12800,128]{1,0:T(8,128)(2,1)S(1)}, u32[]{:S(2)}, u32[]{:S(2)}) collective-permute-start(bf16[12800,128]{1,0:T(8,128)(2,1)S(1)} %collective-permute-done.refs_1_), channel_id=1, source_target_pairs={{0,7},{1,0},{2,1},{3,2},{4,3},{5,4},{6,5},{7,6},{8,15},{9,8},{10,9... | collective-permute-start | bytes 9830408 | tf_op jit(solution)/shard_map/ppermute | solution.py:19
  281.1 39.9 %collective-permute-start.2 = (bf16[12800,128]{1,0:T(8,128)(2,1)S(1)}, bf16[12800,128]{1,0:T(8,128)(2,1)S(1)}, u32[]{:S(2)}, u32[]{:S(2)}) collective-permute-start(bf16[12800,128]{1,0:T(8,128)(2,1)S(1)} %collective-permute-done.1.refs_1_), channel_id=1, source_target_pairs={{0,7},{1,0},{2,1},{3,2},{4,3},{5,4},{6,5},{7,6},{8,15},{9,8},{10,9... | collective-permute-start | bytes 9830408 | tf_op jit(solution)/shard_map/ppermute | solution.py:19
  321.0 39.9 %collective-permute-start.3 = (bf16[12800,128]{1,0:T(8,128)(2,1)S(1)}, bf16[12800,128]{1,0:T(8,128)(2,1)S(1)}, u32[]{:S(2)}, u32[]{:S(2)}) collective-permute-start(bf16[12800,128]{1,0:T(8,128)(2,1)S(1)} %collective-permute-done.2.refs_1_), channel_id=1, source_target_pairs={{0,7},{1,0},{2,1},{3,2},{4,3},{5,4},{6,5},{7,6},{8,15},{9,8},{10,9... | collective-permute-start | bytes 9830408 | tf_op jit(solution)/shard_map/ppermute | solution.py:19

commit v3 on v2

--- a/solution.py
+++ b/solution.py
@@ -11,6 +11,7 @@
 NSPEC = 25
 LANES = 128
 DEPTH = 32
+PARTS = 2
 
 
 def from_behind(value, axis, steps):
@@ -114,10 +115,11 @@
 
 
 def correlate_kernel(inputs, channels, first, *refs):
+    rows, products = refs[-2:]
     if first:
-        partner_ref, out_ref, own_ref, rows, products = refs
+        partner_ref, out_ref, own_ref = refs[0], refs[-4], refs[-3]
     else:
-        own_ref, partner_ref, _, out_ref, rows, products = refs
+        own_ref, partner_ref, out_ref = refs[0], refs[1], refs[-3]
     scale = jnp.float32(1.0 / NSPEC)
     lanes = 2 * inputs
     total = channels * NSPEC
@@ -157,31 +159,37 @@
     lax.fori_loop(0, inputs, turn, 0, unroll=4)
 
 
-def correlate(own, partner, visibility, lag, lag_count, inputs, channel_count):
-    block = min(LANES, channel_count)
+def correlate(own, partner, visibility, lag, lag_count, inputs, channel_count, part, parts):
+    part_channels = channel_count // parts
+    block = min(LANES, part_channels)
+    ahead = part * (part_channels // block)
     out_shape = [
         jax.ShapeDtypeStruct((2, inputs, lag_count, inputs, channel_count), jnp.float32)
     ]
-    out_specs = [pl.BlockSpec((2, inputs, 1, inputs, block), lambda c: (0, 0, lag, 0, c))]
+    out_specs = [pl.BlockSpec((2, inputs, 1, inputs, block), lambda c: (0, 0, lag, 0, ahead + c))]
     own_spec = pl.BlockSpec((block, inputs, 2 * DEPTH), lambda c: (c, 0, 0))
     partner_spec = pl.BlockSpec((block * NSPEC, 2 * inputs), lambda c: (c, 0))
     first = own is None
     if first:
-        in_specs, operands, aliases = [partner_spec], [partner], {}
+        in_specs, operands = [partner_spec], [partner]
         out_shape.append(
-            jax.ShapeDtypeStruct((channel_count, inputs, 2 * DEPTH), jnp.bfloat16)
+            jax.ShapeDtypeStruct((part_channels, inputs, 2 * DEPTH), jnp.bfloat16)
         )
         out_specs.append(own_spec)
     else:
-        in_specs = [own_spec, partner_spec, pl.BlockSpec(memory_space=pl.ANY)]
-        operands, aliases = [own, partner, visibility], {2: 0}
+        in_specs, operands = [own_spec, partner_spec], [own, partner]
+    aliases = {}
+    if visibility is not None:
+        aliases = {len(operands): 0}
+        in_specs.append(pl.BlockSpec(memory_space=pl.ANY))
+        operands.append(visibility)
 
     def kernel(*refs):
         correlate_kernel(inputs, block, first, *refs)
 
     results = pl.pallas_call(
         kernel,
-        grid=(channel_count // block,),
+        grid=(part_channels // block,),
         out_shape=out_shape,
         in_specs=in_specs,
         out_specs=out_specs,
@@ -192,10 +200,77 @@
         input_output_aliases=aliases,
         compiler_params=pltpu.CompilerParams(vmem_limit_bytes=40 * 1024 * 1024),
         cost_estimate=pl.CostEstimate(
-            flops=35_000_000_000, bytes_accessed=24_000_000, transcendentals=0
+            flops=17_000_000_000, bytes_accessed=12_000_000, transcendentals=0
         ),
     )(*operands)
     return (results[0], results[1]) if first else (results[0], own)
+
+
+def regroup_kernel(tm_count, inputs, me_ref, *refs):
+    pieces, out_ref, stage, rows = refs[:-3], refs[-3], refs[-2], refs[-1]
+    per = inputs // tm_count
+    channels = out_ref.shape[0] // NSPEC
+    for k in range(tm_count):
+        source = me_ref[0] ^ k
+        for plane in range(2):
+            place = pl.ds(pl.multiple_of(plane * inputs + source * per, per), per)
+
+            def fill(s, carry, piece=pieces[2 * k + plane], place=place):
+                stage[s, place, :] = piece[s].astype(jnp.float32)
+                return carry
+
+            lax.fori_loop(0, NSPEC, fill, 0, unroll=5)
+
+    def turn(s, carry):
+        rows[pl.ds(s, channels, stride=NSPEC), :] = jnp.transpose(stage[s])
+        return carry
+
+    lax.fori_loop(0, NSPEC, turn, 0, unroll=5)
+    out_ref[...] = rows[...].astype(jnp.bfloat16)
+
+
+def regroup(pieces, me, inputs):
+    tm_count = len(pieces)
+    _, per, columns = pieces[0].shape
+    channels = columns // 2
+    block = min(LANES, channels)
+    blocks = channels // block
+    shape = (NSPEC, per, block)
+    in_specs = [pl.BlockSpec(memory_space=pltpu.SMEM)]
+    operands = [me]
+    for piece in pieces:
+        in_specs.append(pl.BlockSpec(shape, lambda c: (0, 0, c)))
+        in_specs.append(pl.BlockSpec(shape, lambda c: (0, 0, blocks + c)))
+        operands += [piece, piece]
+
+    def kernel(*refs):
+        regroup_kernel(tm_count, inputs, *refs)
+
+    return pl.pallas_call(
+        kernel,
+        grid=(blocks,),
+        out_shape=jax.ShapeDtypeStruct((channels * NSPEC, 2 * inputs), jnp.bfloat16),
+        in_specs=in_specs,
+        out_specs=pl.BlockSpec((block * NSPEC, 2 * inputs), lambda c: (c, 0)),
+        scratch_shapes=[
+            pltpu.VMEM((NSPEC, 2 * inputs, block), jnp.float32),
+            pltpu.VMEM((block * NSPEC, 2 * inputs), jnp.float32),
+        ],
+        compiler_params=pltpu.CompilerParams(vmem_limit_bytes=40 * 1024 * 1024),
+        cost_estimate=pl.CostEstimate(
+            flops=4_000_000_000, bytes_accessed=4_000_000, transcendentals=0
+        ),
+    )(*operands)
+
+
+def exchange(blocks, axis):
+    count = lax.axis_size(axis)
+    me = lax.axis_index(axis)
+    pieces = [lax.dynamic_index_in_dim(blocks, me, 0, keepdims=False)]
+    for k in range(1, count):
+        block = lax.dynamic_index_in_dim(blocks, me ^ k, 0, keepdims=False)
+        pieces.append(lax.ppermute(block, axis, [(d, d ^ k) for d in range(count)]))
+    return pieces
 
 
 def shards(voltages, taper):
@@ -207,31 +282,37 @@
     channel_count = frame_len // 2 // tm_count
     lag_count = stat_count // 2 + 1
     per = local_inputs // tm_count
+    part_channels = channel_count // PARTS
     table = dft_table(segment, channel_count, frame_len, LANES)
+    table = table.reshape(2 * segment, 2, PARTS, part_channels)
+    me = lax.axis_index("tm").astype(jnp.int32).reshape(1)
 
     series = lax.all_to_all(
         voltages.reshape(tm_count, per, samples), "tm", split_axis=0, concat_axis=0, tiled=True
     )
     twisted = channelize(series, taper, LANES)
-    spectra = jnp.dot(
-        twisted.reshape(tm_count * NSPEC * per, 2 * segment),
-        table,
-        precision=lax.Precision.HIGH,
-        preferred_element_type=jnp.float32,
-    ).astype(jnp.bfloat16)
-    spectra = spectra.reshape(tm_count, NSPEC * per, 2 * channel_count)
-    spectra = lax.all_to_all(spectra, "tm", split_axis=0, concat_axis=0, tiled=True)
-    spectra = spectra.reshape(tm_count, NSPEC, per, 2, channel_count)
-    block = jnp.transpose(spectra, (4, 1, 3, 0, 2)).reshape(
-        channel_count * NSPEC, 2 * local_inputs
-    )
-    visibility = own = None
+    twisted = twisted.reshape(tm_count * NSPEC * per, 2 * segment)
+    blocks = []
+    for part in range(PARTS):
+        spectra = jnp.dot(
+            twisted,
+            table[:, :, part].reshape(2 * segment, 2 * part_channels),
+            precision=lax.Precision.HIGH,
+            preferred_element_type=jnp.float32,
+        ).astype(jnp.bfloat16)
+        spectra = spectra.reshape(tm_count, NSPEC, per, 2 * part_channels)
+        blocks.append(regroup(exchange(spectra, "tm"), me, local_inputs))
+    visibility = None
+    own = [None] * PARTS
     for lag in range(lag_count):
-        following = from_behind(block, "stat", -1) if lag < lag_count - 1 else None
-        visibility, own = correlate(
-            own, block, visibility, lag, lag_count, local_inputs, channel_count
-        )
-        block = following
+        for part in range(PARTS):
+            block = blocks[part]
+            if lag < lag_count - 1:
+                blocks[part] = from_behind(block, "stat", -1)
+            visibility, own[part] = correlate(
+                own[part], block, visibility, lag, lag_count, local_inputs, channel_count,
+                part, PARTS,
+            )
     return visibility[None]
 
 

time: 393 us -> 325 us (0.83)
  blocking collectives: 105 us -> 0 us
  waiting for transfers between devices: 15.8 us -> 77.7 us
  local copies, waits for them, and re-layouts: 48.4 us -> 0.35 us
  Pallas kernels: 186 us -> 204 us
  starting transfers between devices: 11.5 us -> 17.5 us
    all_to_all x2 -> x0, blocking collectives: 105 us -> none  [the longest x1 64.8 us: shards(): lax.all_to_all(voltages.reshape(tm_count, per, samples), 'tm', split_axis...]
    all_to_all x0 -> x1, waiting for transfers between devices: none -> 60 us  [shards(): lax.all_to_all(voltages.reshape(tm_count, per, samples), 'tm', split_axis...]
    reshape x3 -> x0, local copies, waits for them, and re-layouts: 33 us -> none  [the longest x2 25.7 us: shards(): jnp.transpose(spectra, (4, 1, 3, 0, 2))]
    ppermute x0 -> x6, waiting for transfers between devices: none -> 17.6 us  [exchange(): pieces.append(lax.ppermute(block, axis, [(d, d ^ k) for d in range(count)]))]
    ppermute x4 -> x8, waiting for transfers between devices: 15.8 us -> 0.02 us  [from_behind(): return lax.ppermute(value, axis, pairs)]
    pallas_call x5 -> x12, Pallas kernels: 169 us -> 185 us  [the longest x10 179 us: correlate(): pl.pallas_call(kernel, grid=(part_channels // block,), out_shape=out_shap...]
    transpose x1 -> x0, local copies, waits for them, and re-layouts: 15.3 us -> none  [shards(): jnp.transpose(spectra, (4, 1, 3, 0, 2))]
    ppermute x0 -> x6, starting transfers between devices: none -> 7.11 us  [exchange(): pieces.append(lax.ppermute(block, axis, [(d, d ^ k) for d in range(count)]))]
  transfers between devices with their start and end apart: 4 -> 15, of which waited for: 3 -> 5; matrix products, arithmetic and copies ran while one was open for 0% -> 3% of each run, Pallas kernels for 35% -> 52%
where the time goes in v3:
time: 325 us
  Pallas kernels  204 us (63%)
  waiting for transfers between devices  77.7 us (24%)
  matrix products  25.3 us (8%)
  starting transfers between devices  17.5 us (5%)
    pallas_call x10, Pallas kernels, correlate(): pl.pallas_call(kernel, grid=(part_channels // block,), out_shape=out_shap...  179 us
    all_to_all x1, waiting for transfers between devices, shards(): lax.all_to_all(voltages.reshape(tm_count, per, samples), 'tm', split_axis...  60 us
    dot_general x2, matrix products, shards(): jnp.dot(twisted, table[:, :, part].reshape(2 * segment, 2 * part_channels...  25.3 us
    pallas_call x1, Pallas kernels, channelize(): pl.pallas_call(kernel, grid=(segment // width,), out_shape=jax.ShapeDtype...  19.4 us
    ppermute x6, waiting for transfers between devices, exchange(): pieces.append(lax.ppermute(block, axis, [(d, d ^ k) for d in range(count)]))  17.6 us
    ppermute x6, starting transfers between devices, exchange(): pieces.append(lax.ppermute(block, axis, [(d, d ^ k) for d in range(count)]))  7.11 us
  transfers between devices with their start and end apart: 15, of which 5 were waited for; matrix products, arithmetic and copies ran while one was open for 3% of the time, Pallas kernels for 52%

profile of v3, /device:TPU:0, one launch (start us, length us, event | category | flops | bytes accessed | tf_op | source)
XLA Modules:
  0.0 325.3 jit_solution(6507291497632542862)
XLA Ops:
  0.0 5.3 %all-to-all-start = ((bf16[4,16,40960]{2,1,0:T(8,128)(2,1)}), bf16[4,16,40960]{2,1,0:T(8,128)(2,1)}, u32[]{:S(2)}, u32[]{:S(2)}) async-start(bf16[4,16,40960]{2,1,0:T(8,128)(2,1)} %bitcast.28), calls=%async_computation | async-start | bytes 10485760 | tf_op jit(solution)/shard_map/all_to_all | solution.py:290
  5.3 60.0 %all-to-all-done.refs_0_ = bf16[4,16,40960]{2,1,0:T(8,128)(2,1)} async-done(((bf16[4,16,40960]{2,1,0:T(8,128)(2,1)}), bf16[4,16,40960]{2,1,0:T(8,128)(2,1)}, u32[]{:S(2)}, u32[]{:S(2)}) %all-to-all-start) | async-done | bytes 5242912 | tf_op jit(solution)/shard_map/all_to_all | solution.py:290
  65.3 19.4 %shard_map.64 = f32[4,25,16,2048]{3,2,1,0:T(8,128)} custom-call(bf16[4,16,40960]{2,1,0:T(8,128)(2,1)} %all-to-all-done.refs_0_, f32[16,4096]{1,0:T(8,128)S(1)} %copy-done, f32[4,1024]{1,0:T(4,128)S(1)} %copy-done.1, f32[4,1024]{1,0:T(4,128)S(1)} %copy-done.2), custom_call_target="tpu_custom_call" | custom-call | flops 200000000 | bytes 20000000 | tf_op jit(solution)/shard_map/pallas_call | solution.py:98
  84.7 14.8 %convolution_convert_fusion = bf16[1600,512]{1,0:T(8,128)(2,1)S(1)} fusion(f32[1600,2048]{1,0:T(8,128)} %bitcast.26, f32[2048,512]{1,0:T(8,128)} %constant.41.clone), kind=kOutput, calls=%fused_computation | convolution fusion | flops 10067148800 | bytes 18939904 | tf_op jit(solution)/shard_map/dot_general | solution.py:297
  99.7 1.6 collective-permute-start.3
  103.3 10.4 %convolution_convert_fusion.1 = bf16[1600,512]{1,0:T(8,128)(2,1)S(1)} fusion(f32[1600,2048]{1,0:T(8,128)S(1)} %bitcast.27, f32[2048,512]{1,0:T(8,128)S(1)} %copy-done.4), kind=kOutput, calls=%fused_computation.1 | convolution fusion | flops 10067148800 | bytes 18939904 | tf_op jit(solution)/shard_map/dot_general | solution.py:297
  113.9 1.6 collective-permute-start
  115.9 1.5 collective-permute-start.2
  118.9 3.1 collective-permute-done.5.refs_7_.refs_8_
  122.0 2.8 shard_map.66.refs_0_
  124.8 5.0 %collective-permute-done.refs_3_.refs_4_ = bf16[25,16,512]{2,1,0:T(8,128)(2,1)S(1)} collective-permute-done((bf16[25,16,512]{2,1,0:T(8,128)(2,1)S(1)}, bf16[25,16,512]{2,1,0:T(8,128)(2,1)S(1)}, u32[]{:S(2)}, u32[]{:S(2)}) %collective-permute-start) | collective-permute-done | bytes 409632 | tf_op jit(solution)/shard_map/ppermute | solution.py:272
  129.8 8.2 %collective-permute-done.1.refs_5_.refs_6_ = bf16[25,16,512]{2,1,0:T(8,128)(2,1)S(1)} collective-permute-done((bf16[25,16,512]{2,1,0:T(8,128)(2,1)S(1)}, bf16[25,16,512]{2,1,0:T(8,128)(2,1)S(1)}, u32[]{:S(2)}, u32[]{:S(2)}) %collective-permute-start.1) | collective-permute-done | bytes 409632 | tf_op jit(solution)/shard_map/ppermute | solution.py:272
  137.9 2.8 shard_map.65.refs_0_
  142.1 23.9 %shard_map.67 = (f32[2,64,5,64,512]{4,3,2,1,0:T(8,128)}, bf16[256,64,64]{2,1,0:T(8,128)(2,1)S(1)}) custom-call(bf16[6400,128]{1,0:T(8,128)(2,1)S(1)} %shard_map.66.refs_0_), custom_call_target="tpu_custom_call" | custom-call | flops 16999999488 | bytes 12000000 | tf_op jit(solution)/shard_map/pallas_call | solution.py:190
  165.9 23.9 %shard_map.68 = (f32[2,64,5,64,512]{4,3,2,1,0:T(8,128)}, bf16[256,64,64]{2,1,0:T(8,128)(2,1)S(1)}) custom-call(bf16[6400,128]{1,0:T(8,128)(2,1)S(1)} %shard_map.65.refs_0_, f32[2,64,5,64,512]{4,3,2,1,0:T(8,128)} %get-tuple-element.9.refs_1_), custom_call_target="tpu_custom_call", output_to_operand_aliasing={{0}: (1, {})} | custom-call | flops 16999999488 | bytes 12000000 | tf_op jit(solution)/shard_map/pallas_call | solution.py:190
  189.8 2.5 collective-permute-start.11
  192.4 16.5 %shard_map.69.refs_2_ = f32[2,64,5,64,512]{4,3,2,1,0:T(8,128)} custom-call(bf16[256,64,64]{2,1,0:T(8,128)(2,1)S(1)} %get-tuple-element.11.refs_0_, bf16[6400,128]{1,0:T(8,128)(2,1)S(1)} %collective-permute-done.10.refs_1_, f32[2,64,5,64,512]{4,3,2,1,0:T(8,128)} %get-tuple-element.12.refs_2_), custom_call_target="tpu_custom_call", output_to_operand_aliasing={{}: (2, {})} | custom-call | flops 16999999488 | bytes 12000000 | tf_op jit(solution)/shard_map/pallas_call | solution.py:190
  208.9 16.5 %shard_map.70.refs_2_ = f32[2,64,5,64,512]{4,3,2,1,0:T(8,128)} custom-call(bf16[256,64,64]{2,1,0:T(8,128)(2,1)S(1)} %get-tuple-element.10.refs_0_, bf16[6400,128]{1,0:T(8,128)(2,1)S(1)} %collective-permute-done.6.refs_1_, f32[2,64,5,64,512]{4,3,2,1,0:T(8,128)} %shard_map.69.refs_2_), custom_call_target="tpu_custom_call", output_to_operand_aliasing={{}: (2, {})} | custom-call | flops 16999999488 | bytes 12000000 | tf_op jit(solution)/shard_map/pallas_call | solution.py:190
  225.8 16.5 %shard_map.71.refs_2_ = f32[2,64,5,64,512]{4,3,2,1,0:T(8,128)} custom-call(bf16[256,64,64]{2,1,0:T(8,128)(2,1)S(1)} %get-tuple-element.11.refs_0_, bf16[6400,128]{1,0:T(8,128)(2,1)S(1)} %collective-permute-done.11.refs_1_, f32[2,64,5,64,512]{4,3,2,1,0:T(8,128)} %shard_map.70.refs_2_), custom_call_target="tpu_custom_call", output_to_operand_aliasing={{}: (2, {})} | custom-call | flops 16999999488 | bytes 12000000 | tf_op jit(solution)/shard_map/pallas_call | solution.py:190
  242.4 16.5 %shard_map.72.refs_2_ = f32[2,64,5,64,512]{4,3,2,1,0:T(8,128)} custom-call(bf16[256,64,64]{2,1,0:T(8,128)(2,1)S(1)} %get-tuple-element.10.refs_0_, bf16[6400,128]{1,0:T(8,128)(2,1)S(1)} %collective-permute-done.7.refs_1_, f32[2,64,5,64,512]{4,3,2,1,0:T(8,128)} %shard_map.71.refs_2_), custom_call_target="tpu_custom_call", output_to_operand_aliasing={{}: (2, {})} | custom-call | flops 16999999488 | bytes 12000000 | tf_op jit(solution)/shard_map/pallas_call | solution.py:190
  259.3 16.5 %shard_map.73.refs_2_ = f32[2,64,5,64,512]{4,3,2,1,0:T(8,128)} custom-call(bf16[256,64,64]{2,1,0:T(8,128)(2,1)S(1)} %get-tuple-element.11.refs_0_, bf16[6400,128]{1,0:T(8,128)(2,1)S(1)} %collective-permute-done.12.refs_1_, f32[2,64,5,64,512]{4,3,2,1,0:T(8,128)} %shard_map.72.refs_2_), custom_call_target="tpu_custom_call", output_to_operand_aliasing={{}: (2, {})} | custom-call | flops 16999999488 | bytes 12000000 | tf_op jit(solution)/shard_map/pallas_call | solution.py:190
  275.9 16.5 %shard_map.74.refs_2_ = f32[2,64,5,64,512]{4,3,2,1,0:T(8,128)} custom-call(bf16[256,64,64]{2,1,0:T(8,128)(2,1)S(1)} %get-tuple-element.10.refs_0_, bf16[6400,128]{1,0:T(8,128)(2,1)S(1)} %collective-permute-done.8.refs_1_, f32[2,64,5,64,512]{4,3,2,1,0:T(8,128)} %shard_map.73.refs_2_), custom_call_target="tpu_custom_call", output_to_operand_aliasing={{}: (2, {})} | custom-call | flops 16999999488 | bytes 12000000 | tf_op jit(solution)/shard_map/pallas_call | solution.py:190
  292.3 16.5 %shard_map.75.refs_2_ = f32[2,64,5,64,512]{4,3,2,1,0:T(8,128)} custom-call(bf16[256,64,64]{2,1,0:T(8,128)(2,1)S(1)} %get-tuple-element.11.refs_0_, bf16[6400,128]{1,0:T(8,128)(2,1)S(1)} %collective-permute-done.13.refs_1_, f32[2,64,5,64,512]{4,3,2,1,0:T(8,128)} %shard_map.74.refs_2_), custom_call_target="tpu_custom_call", output_to_operand_aliasing={{}: (2, {})} | custom-call | flops 16999999488 | bytes 12000000 | tf_op jit(solution)/shard_map/pallas_call | solution.py:190
  308.8 16.5 %shard_map.76 = f32[2,64,5,64,512]{4,3,2,1,0:T(8,128)} custom-call(bf16[256,64,64]{2,1,0:T(8,128)(2,1)S(1)} %get-tuple-element.10.refs_0_, bf16[6400,128]{1,0:T(8,128)(2,1)S(1)} %collective-permute-done.9.refs_1_, f32[2,64,5,64,512]{4,3,2,1,0:T(8,128)} %shard_map.75.refs_2_), custom_call_target="tpu_custom_call", output_to_operand_aliasing={{}: (2, {})} | custom-call | flops 16999999488 | bytes 12000000 | tf_op jit(solution)/shard_map/pallas_call | solution.py:190
  (33 shorter events, 6.9 us)
Async XLA Ops:
  0.0 65.3 %copy-start = (f32[16,4096]{1,0:T(8,128)S(1)}, f32[16,4096]{1,0:T(8,128)}, u32[]{:S(2)}) copy-start(f32[16,4096]{1,0:T(8,128)} %refs_1_.1) | copy-start | bytes 786436
  0.0 65.3 %copy-start.1 = (f32[4,1024]{1,0:T(4,128)S(1)}, f32[4,1024]{1,0:T(4,128)}, u32[]{:S(2)}) copy-start(f32[4,1024]{1,0:T(4,128)} %constant.39.clone.refs_2_) | copy-start | bytes 49156
  0.0 65.3 %copy-start.2 = (f32[4,1024]{1,0:T(4,128)S(1)}, f32[4,1024]{1,0:T(4,128)}, u32[]{:S(2)}) copy-start(f32[4,1024]{1,0:T(4,128)} %constant.40.clone.refs_3_) | copy-start | bytes 49156
  0.0 65.3 %all-to-all-start = ((bf16[4,16,40960]{2,1,0:T(8,128)(2,1)}), bf16[4,16,40960]{2,1,0:T(8,128)(2,1)}, u32[]{:S(2)}, u32[]{:S(2)}) async-start(bf16[4,16,40960]{2,1,0:T(8,128)(2,1)} %bitcast.28), calls=%async_computation | async-start | bytes 10485760 | tf_op jit(solution)/shard_map/all_to_all | solution.py:290
  84.7 18.6 %copy-start.3 = (f32[4,25,16,2048]{3,2,1,0:T(8,128)S(1)}, f32[4,25,16,2048]{3,2,1,0:T(8,128)}, u32[]{:S(2)}) copy-start(f32[4,25,16,2048]{3,2,1,0:T(8,128)} %shard_map.64) | copy-start | bytes 39321604
  84.7 18.6 %copy-start.4 = (f32[2048,512]{1,0:T(8,128)S(1)}, f32[2048,512]{1,0:T(8,128)}, u32[]{:S(2)}) copy-start(f32[2048,512]{1,0:T(8,128)} %constant.42.clone) | copy-start | bytes 12582916
  99.7 16.2 %collective-permute-start.3 = (bf16[25,16,512]{2,1,0:T(8,128)(2,1)S(1)}, bf16[25,16,512]{2,1,0:T(8,128)(2,1)S(1)}, u32[]{:S(2)}, u32[]{:S(2)}) collective-permute-start(bf16[25,16,512]{2,1,0:T(8,128)(2,1)S(1)} %get-tuple-element.15), channel_id=1, source_target_pairs={{0,8},{8,0},{16,24},{24,16},{1,9},{9,1},{17,25},{25,17},{2,10},{10... | collective-permute-start | bytes 1228808 | tf_op jit(solution)/shard_map/ppermute | solution.py:272
  101.3 17.6 %collective-permute-start.4 = (bf16[25,16,512]{2,1,0:T(8,128)(2,1)S(1)}, bf16[25,16,512]{2,1,0:T(8,128)(2,1)S(1)}, u32[]{:S(2)}, u32[]{:S(2)}) collective-permute-start(bf16[25,16,512]{2,1,0:T(8,128)(2,1)S(1)} %get-tuple-element.14), channel_id=1, source_target_pairs={{0,16},{8,24},{16,0},{24,8},{1,17},{9,25},{17,1},{25,9},{2,18},{10... | collective-permute-start | bytes 1228808 | tf_op jit(solution)/shard_map/ppermute | solution.py:272
  101.8 20.2 %collective-permute-start.5 = (bf16[25,16,512]{2,1,0:T(8,128)(2,1)S(1)}, bf16[25,16,512]{2,1,0:T(8,128)(2,1)S(1)}, u32[]{:S(2)}, u32[]{:S(2)}) collective-permute-start(bf16[25,16,512]{2,1,0:T(8,128)(2,1)S(1)} %get-tuple-element.13), channel_id=1, source_target_pairs={{0,24},{8,16},{16,8},{24,0},{1,25},{9,17},{17,9},{25,1},{2,26},{10... | collective-permute-start | bytes 1228808 | tf_op jit(solution)/shard_map/ppermute | solution.py:272
  113.9 15.9 %collective-permute-start = (bf16[25,16,512]{2,1,0:T(8,128)(2,1)S(1)}, bf16[25,16,512]{2,1,0:T(8,128)(2,1)S(1)}, u32[]{:S(2)}, u32[]{:S(2)}) collective-permute-start(bf16[25,16,512]{2,1,0:T(8,128)(2,1)S(1)} %get-tuple-element.19), channel_id=1, source_target_pairs={{0,8},{8,0},{16,24},{24,16},{1,9},{9,1},{17,25},{25,17},{2,10},{10... | collective-permute-start | bytes 1228808 | tf_op jit(solution)/shard_map/ppermute | solution.py:272
  115.4 22.5 %collective-permute-start.1 = (bf16[25,16,512]{2,1,0:T(8,128)(2,1)S(1)}, bf16[25,16,512]{2,1,0:T(8,128)(2,1)S(1)}, u32[]{:S(2)}, u32[]{:S(2)}) collective-permute-start(bf16[25,16,512]{2,1,0:T(8,128)(2,1)S(1)} %get-tuple-element.18), channel_id=1, source_target_pairs={{0,16},{8,24},{16,0},{24,8},{1,17},{9,25},{17,1},{25,9},{2,18},{10... | collective-permute-start | bytes 1228808 | tf_op jit(solution)/shard_map/ppermute | solution.py:272
  115.9 22.0 %collective-permute-start.2 = (bf16[25,16,512]{2,1,0:T(8,128)(2,1)S(1)}, bf16[25,16,512]{2,1,0:T(8,128)(2,1)S(1)}, u32[]{:S(2)}, u32[]{:S(2)}) collective-permute-start(bf16[25,16,512]{2,1,0:T(8,128)(2,1)S(1)} %get-tuple-element.17), channel_id=1, source_target_pairs={{0,24},{8,16},{16,8},{24,0},{1,25},{9,17},{17,9},{25,1},{2,26},{10... | collective-permute-start | bytes 1228808 | tf_op jit(solution)/shard_map/ppermute | solution.py:272
  124.7 65.1 %collective-permute-start.10 = (bf16[6400,128]{1,0:T(8,128)(2,1)S(1)}, bf16[6400,128]{1,0:T(8,128)(2,1)S(1)}, u32[]{:S(2)}, u32[]{:S(2)}) collective-permute-start(bf16[6400,128]{1,0:T(8,128)(2,1)S(1)} %shard_map.66.refs_0_), channel_id=1, source_target_pairs={{0,7},{1,0},{2,1},{3,2},{4,3},{5,4},{6,5},{7,6},{8,15},{9,8},{10,9... | collective-permute-start | bytes 4915208 | tf_op jit(solution)/shard_map/ppermute | solution.py:20
  140.7 51.6 %collective-permute-start.6 = (bf16[6400,128]{1,0:T(8,128)(2,1)S(1)}, bf16[6400,128]{1,0:T(8,128)(2,1)S(1)}, u32[]{:S(2)}, u32[]{:S(2)}) collective-permute-start(bf16[6400,128]{1,0:T(8,128)(2,1)S(1)} %shard_map.65.refs_0_), channel_id=1, source_target_pairs={{0,7},{1,0},{2,1},{3,2},{4,3},{5,4},{6,5},{7,6},{8,15},{9,8},{10,9... | collective-permute-start | bytes 4915208 | tf_op jit(solution)/shard_map/ppermute | solution.py:20
  189.8 35.5 %collective-permute-start.11 = (bf16[6400,128]{1,0:T(8,128)(2,1)S(1)}, bf16[6400,128]{1,0:T(8,128)(2,1)S(1)}, u32[]{:S(2)}, u32[]{:S(2)}) collective-permute-start(bf16[6400,128]{1,0:T(8,128)(2,1)S(1)} %collective-permute-done.10.refs_1_), channel_id=1, source_target_pairs={{0,7},{1,0},{2,1},{3,2},{4,3},{5,4},{6,5},{7,6},{8,15},{9,8},{10,9... | collective-permute-start | bytes 4915208 | tf_op jit(solution)/shard_map/ppermute | solution.py:20
  192.3 50.0 %collective-permute-start.7 = (bf16[6400,128]{1,0:T(8,128)(2,1)S(1)}, bf16[6400,128]{1,0:T(8,128)(2,1)S(1)}, u32[]{:S(2)}, u32[]{:S(2)}) collective-permute-start(bf16[6400,128]{1,0:T(8,128)(2,1)S(1)} %collective-permute-done.6.refs_1_), channel_id=1, source_target_pairs={{0,7},{1,0},{2,1},{3,2},{4,3},{5,4},{6,5},{7,6},{8,15},{9,8},{10,9... | collective-permute-start | bytes 4915208 | tf_op jit(solution)/shard_map/ppermute | solution.py:20
  225.3 33.5 %collective-permute-start.12 = (bf16[6400,128]{1,0:T(8,128)(2,1)S(1)}, bf16[6400,128]{1,0:T(8,128)(2,1)S(1)}, u32[]{:S(2)}, u32[]{:S(2)}) collective-permute-start(bf16[6400,128]{1,0:T(8,128)(2,1)S(1)} %collective-permute-done.11.refs_1_), channel_id=1, source_target_pairs={{0,7},{1,0},{2,1},{3,2},{4,3},{5,4},{6,5},{7,6},{8,15},{9,8},{10,9... | collective-permute-start | bytes 4915208 | tf_op jit(solution)/shard_map/ppermute | solution.py:20
  242.3 33.5 %collective-permute-start.8 = (bf16[6400,128]{1,0:T(8,128)(2,1)S(1)}, bf16[6400,128]{1,0:T(8,128)(2,1)S(1)}, u32[]{:S(2)}, u32[]{:S(2)}) collective-permute-start(bf16[6400,128]{1,0:T(8,128)(2,1)S(1)} %collective-permute-done.7.refs_1_), channel_id=1, source_target_pairs={{0,7},{1,0},{2,1},{3,2},{4,3},{5,4},{6,5},{7,6},{8,15},{9,8},{10,9... | collective-permute-start | bytes 4915208 | tf_op jit(solution)/shard_map/ppermute | solution.py:20
  258.8 33.5 %collective-permute-start.13 = (bf16[6400,128]{1,0:T(8,128)(2,1)S(1)}, bf16[6400,128]{1,0:T(8,128)(2,1)S(1)}, u32[]{:S(2)}, u32[]{:S(2)}) collective-permute-start(bf16[6400,128]{1,0:T(8,128)(2,1)S(1)} %collective-permute-done.12.refs_1_), channel_id=1, source_target_pairs={{0,7},{1,0},{2,1},{3,2},{4,3},{5,4},{6,5},{7,6},{8,15},{9,8},{10,9... | collective-permute-start | bytes 4915208 | tf_op jit(solution)/shard_map/ppermute | solution.py:20
  275.8 33.0 %collective-permute-start.9 = (bf16[6400,128]{1,0:T(8,128)(2,1)S(1)}, bf16[6400,128]{1,0:T(8,128)(2,1)S(1)}, u32[]{:S(2)}, u32[]{:S(2)}) collective-permute-start(bf16[6400,128]{1,0:T(8,128)(2,1)S(1)} %collective-permute-done.8.refs_1_), channel_id=1, source_target_pairs={{0,7},{1,0},{2,1},{3,2},{4,3},{5,4},{6,5},{7,6},{8,15},{9,8},{10,9... | collective-permute-start | bytes 4915208 | tf_op jit(solution)/shard_map/ppermute | solution.py:20
